TPU v7x, 32 devices: a whole 2x2x4 slice. The times are simulated.
32 devices in a mesh: dp: 8 (over z, y), fsdp: 4 (over x, core).
Axes of the slice: x: 2, y: 2, z: 4, core: 2. Of those that a mesh axis runs over, the one named last changes fastest.
Arguments:
- drafts: bfloat16 [1024, 2048], P(('dp', 'fsdp')), may hold values from -6 to 6
- cache: bfloat16 [32, 2, 768, 1024], P(('dp', 'fsdp')), may hold values from -7 to 7
- cache_len: int32 [32], P(('dp', 'fsdp')), may hold values from 2 to 768, as said below
- parents: int32 [32, 32], P(('dp', 'fsdp')), may hold values from 0 to 30, as said below
- accepted: int32 [32], P(('dp', 'fsdp')), may hold values from 0 to 31
- order: int32 [32], replicated, may hold values from 0 to 31, each once
- attn_gain: float32 [2048], replicated, may hold values from 0.5 to 1.5
- w_qkv: bfloat16 [2048, 3072], P(None, 'fsdp'), may hold values from -0.125 to 0.125
- qkv_bias: float32 [3072], replicated, may hold values from -5 to 5
- w_out: bfloat16 [1024, 2048], P(None, 'fsdp'), may hold values from -0.1875 to 0.1875
- moe_gain: float32 [2048], replicated, may hold values from 0.5 to 1.5
- router: bfloat16 [2048, 8], replicated, may hold values from -0.125 to 0.125
- expert_ids: int32 [1024, 4], P('dp'), may hold values from 0 to 7, all different within a row; in each aligned block of 128 rows (0 to 127, 128 to 255, ...) at most 128 rows name the same one
- w_gate_up: bfloat16 [8, 2, 2048, 1408], P('dp', None, None, 'fsdp'), may hold values from -0.125 to 0.125
- w_down: bfloat16 [8, 1408, 2048], P('dp', 'fsdp'), may hold values from -0.15625 to 0.15625
Outputs:
- layer_out: bfloat16 [1024, 2048], P(('dp', 'fsdp'))
- appended: bfloat16 [32, 2, 32, 1024], P(('dp', 'fsdp'))
- last_state: bfloat16 [32, 2048], replicated
Inputs may be any that keep to these rules, and one draw needn't show every extreme that they name: `cache_len`: some request has all 768 slots valid. parents[r, 0] is 0, and parents[r, i] < i for every node i >= 1. `expert_ids`: each row names 4 different experts; among the 128 rows of one index of dp no expert is named more than 128 times, and in some of them one expert exactly 128 times.
All inputs are finite; a program needn't handle non-finite values.
Results may differ from a plain program's by a relative error of at most 0.014.
Values may be sent and summed in bfloat16 or wider, within the bound.
A program may use at most 128 MiB of HBM per device.

v0:
```python
import math

import jax
import jax.numpy as jnp
from jax import lax
from jax.sharding import PartitionSpec as P

D = 2048
HEADS = 8
HD = 128
TREE = 32


EPS = 1e-06


def scaled_norm(values, gain):
    wide = values.astype(jnp.float32)
    factor = lax.rsqrt(jnp.mean(wide * wide, axis=-1, keepdims=True) + EPS)
    return (wide * factor * gain).astype(jnp.bfloat16)


def ancestors(parent_row):
    count = parent_row.shape[0]
    index = jnp.arange(count, dtype=jnp.int32)
    links = (index[:, None] == index[None, :]) | (parent_row[:, None] == index[None, :])
    closure = links.astype(jnp.float32)
    for level in range((count - 1).bit_length()):
        closure = jnp.minimum(jnp.dot(closure, closure, precision=lax.Precision.HIGHEST), 1.0)
    return closure


def attend(block, cache_block, valid_slots, closure):
    query = block[:, :, 0]
    tree_keys = block[:, :, 1]
    tree_values = block[:, :, 2]
    slots = cache_block.shape[1]
    cache_keys = cache_block[0].reshape(slots, HEADS, HD)
    cache_values = cache_block[1].reshape(slots, HEADS, HD)
    factor = 1.0 / math.sqrt(HD)
    cache_scores = (
        jnp.einsum("thd,chd->htc", query, cache_keys, preferred_element_type=jnp.float32) * factor
    )
    position = jnp.arange(slots, dtype=jnp.int32)
    cache_scores = jnp.where(position[None, None, :] < valid_slots, cache_scores, -1e30)
    tree_scores = (
        jnp.einsum("thd,shd->hts", query, tree_keys, preferred_element_type=jnp.float32) * factor
    )
    tree_scores = jnp.where(closure[None] > 0.5, tree_scores, -1e30)
    top = jnp.maximum(jnp.max(cache_scores, axis=-1), jnp.max(tree_scores, axis=-1))[..., None]
    cache_exp = jnp.exp(cache_scores - top)
    tree_exp = jnp.exp(tree_scores - top)
    total = jnp.sum(cache_exp, axis=-1, keepdims=True) + jnp.sum(tree_exp, axis=-1, keepdims=True)
    cache_weights = (cache_exp / total).astype(jnp.bfloat16)
    tree_weights = (tree_exp / total).astype(jnp.bfloat16)
    mixed = jnp.einsum(
        "htc,chd->thd", cache_weights, cache_values, preferred_element_type=jnp.float32
    )
    mixed = mixed + jnp.einsum(
        "hts,shd->thd", tree_weights, tree_values, preferred_element_type=jnp.float32
    )
    return mixed.astype(jnp.bfloat16).reshape(block.shape[0], HEADS * HD)


def compact(closure, accepted_node, block):
    count = closure.shape[0]
    depth = jnp.sum(closure, axis=1) - 1.0
    on_path = lax.dynamic_index_in_dim(closure, accepted_node, 0, keepdims=False)
    levels = jnp.arange(count, dtype=jnp.int32).astype(jnp.float32)
    select = (on_path[None, :] * (depth[None, :] == levels[:, None]).astype(jnp.float32)).astype(
        jnp.bfloat16
    )
    tree_keys = block[:, :, 1].reshape(count, HEADS * HD)
    tree_values = block[:, :, 2].reshape(count, HEADS * HD)
    kept_keys = jnp.dot(select, tree_keys, preferred_element_type=jnp.float32).astype(jnp.bfloat16)
    kept_values = jnp.dot(select, tree_values, preferred_element_type=jnp.float32).astype(
        jnp.bfloat16
    )
    return jnp.stack([kept_keys, kept_values])


def slots_of(group_ids, experts):
    flat = group_ids.reshape(-1)
    onehot = (flat[:, None] == jnp.arange(experts, dtype=jnp.int32)[None, :]).astype(jnp.int32)
    earlier = jnp.cumsum(onehot, axis=0) - onehot
    return jnp.sum(earlier * onehot, axis=1)


def expert_math(received, w_gate_up, w_down):
    gate_up = jnp.einsum(
        "gecd,ekdf->kgecf", received, w_gate_up, preferred_element_type=jnp.float32
    )
    hidden = (jax.nn.silu(gate_up[0]) * gate_up[1]).astype(jnp.bfloat16)
    return jnp.einsum("gecf,efd->gecd", hidden, w_down, preferred_element_type=jnp.float32).astype(
        jnp.bfloat16
    )


def per_device(
    drafts,
    cache,
    cache_len,
    parents,
    accepted,
    order,
    attn_gain,
    w_qkv,
    qkv_bias,
    w_out,
    moe_gain,
    router,
    expert_ids,
    w_gate_up,
    w_down,
):
    rows = drafts.shape[0]
    requests = cache.shape[0]
    feature = HEADS * HD
    normed = scaled_norm(drafts, attn_gain)
    wide_qkv = lax.all_gather(w_qkv, "fsdp", axis=1, tiled=True)
    full_qkv = jnp.dot(normed, wide_qkv, preferred_element_type=jnp.float32)
    qkv = (full_qkv + qkv_bias).astype(jnp.bfloat16).reshape(rows, HEADS, 3, HD)
    qkv = qkv.reshape(requests, TREE, HEADS, 3, HD)

    def per_request(block, cache_block, valid_slots, parent_row, accepted_node):
        closure = ancestors(parent_row)
        return (
            attend(block, cache_block, valid_slots, closure),
            compact(closure, accepted_node, block),
        )

    attn, appended = jax.vmap(per_request)(qkv, cache, cache_len, parents, accepted)
    attn = attn.reshape(rows, feature)
    wide_out = lax.all_gather(w_out, "fsdp", axis=1, tiled=True)
    projected = jnp.dot(attn, wide_out, preferred_element_type=jnp.float32)
    resid = (drafts.astype(jnp.float32) + projected).astype(jnp.bfloat16)
    moe_input = scaled_norm(resid, moe_gain)
    group_input = lax.all_gather(moe_input, "fsdp", axis=0, tiled=True)
    group_rows = group_input.shape[0]
    experts = router.shape[1]
    chosen_count = expert_ids.shape[1]
    logits = jnp.dot(group_input, router, preferred_element_type=jnp.float32)
    gates = jax.nn.sigmoid(jnp.take_along_axis(logits, expert_ids, axis=1))
    slots = slots_of(expert_ids, experts)
    capacity = 2 * group_rows * chosen_count // experts
    flat_expert = expert_ids.reshape(-1)
    token_index = jnp.arange(group_rows * chosen_count, dtype=jnp.int32) // chosen_count
    buffer = (
        jnp.zeros((experts, capacity, D), jnp.bfloat16)
        .at[flat_expert, slots]
        .set(group_input[token_index])
    )
    local_experts = w_gate_up.shape[0]
    buffer = buffer.reshape(experts // local_experts, local_experts, capacity, D)
    parts = expert_math(
        lax.all_to_all(buffer, "dp", split_axis=0, concat_axis=0, tiled=True), w_gate_up, w_down
    )
    returned = lax.all_to_all(parts, "dp", split_axis=0, concat_axis=0, tiled=True)
    picked = returned.reshape(experts * capacity, D)[flat_expert * capacity + slots]
    weighted = jnp.sum(
        picked.astype(jnp.float32).reshape(group_rows, chosen_count, D) * gates[:, :, None], axis=1
    )
    moe = lax.psum_scatter(weighted, "fsdp", scatter_dimension=0, tiled=True)
    layer_out = (resid.astype(jnp.float32) + moe).astype(jnp.bfloat16)
    final_rows = layer_out.reshape(requests, TREE, D)
    last_rows = jnp.take_along_axis(final_rows, accepted[:, None, None], axis=1)[:, 0]
    everyone = lax.all_gather(last_rows, ("dp", "fsdp"), axis=0, tiled=True)
    last_state = jnp.zeros_like(everyone).at[order].set(everyone)
    return (layer_out, appended, last_state)


def solution(mesh):
    placed = (
        P(("dp", "fsdp"), None),
        P(("dp", "fsdp"), None, None, None),
        P(("dp", "fsdp")),
        P(("dp", "fsdp"), None),
        P(("dp", "fsdp")),
        P(),
        P(),
        P(None, "fsdp"),
        P(),
        P(None, "fsdp"),
        P(),
        P(),
        P("dp", None),
        P("dp", None, None, "fsdp"),
        P("dp", "fsdp", None),
    )
    return jax.shard_map(
        per_device,
        mesh=mesh,
        in_specs=placed,
        out_specs=(P(("dp", "fsdp"), None), P(("dp", "fsdp"), None, None, None), P()),
        check_vma=False,
    )
```

profile of v0, /device:TPU:0, one launch (start us, length us, event | category | flops | bytes accessed | tf_op | source)
XLA Modules:
  0.0 536.2 jit_solution(14828578194772857844)
XLA Ops:
  7.2 0.7 all-gather.4.cloned.1.call-update
  8.0 0.7 all-gather.6.cloned.1.call-update
  9.8 0.8 broadcast_compare_fusion
  11.2 3.8 fusion.63
  15.1 2.6 copy.111
  18.4 2.8 copy.113
  21.1 1.1 reduce-window.6
  23.4 71.1 %all-gather.4.cloned.1.call-done = bf16[2048,3072]{1,0:T(8,128)(2,1)} async-done(((bf16[2048,768]{1,0:T(8,128)(2,1)}), bf16[2048,3072]{1,0:T(8,128)(2,1)}) %all-gather.4.cloned.1.call-update) | async-done | bytes 12582928 | tf_op jit(solution)/shard_map/all_gather | solution.py:120
  94.5 6.9 %fusion.2 = bf16[32,3072]{1,0:T(8,128)(2,1)S(1)} fusion(bf16[2048,3072]{1,0:T(8,128)(2,1)} %all-gather.4.cloned.1.call-done, f32[3072]{0:T(1024)S(1)} %copy-done.11, bf16[32,2048]{1,0:T(8,128)(2,1)S(1)} %copy-done.4, f32[2048]{0:T(1024)S(1)} %copy-done.7, f32[32]{0:T(128)S(1)} %add_rsqrt_fusion.1), kind=kOutput, calls=%fused_computation.10 | convolution fusion | flops 403111936 | bytes 12931200 | tf_op jit(solution)/shard_map/dot_general | solution.py:121
  101.7 0.9 slice_reduce_fusion.2
  102.6 0.9 fusion.65
  103.5 2.0 fusion.64
  106.8 23.8 %all-gather.6.cloned.1.call-done = bf16[1024,2048]{1,0:T(8,128)(2,1)} async-done(((bf16[1024,512]{1,0:T(8,128)(2,1)}), bf16[1024,2048]{1,0:T(8,128)(2,1)}) %all-gather.6.cloned.1.call-update) | async-done | bytes 4194320 | tf_op jit(solution)/shard_map/all_gather | solution.py:134
  130.5 3.1 multiply_reduce_fusion.1
  133.7 0.7 copy-done.2
  134.5 7.2 %all_gather.14 = bf16[128,2048]{1,0:T(8,128)(2,1)S(1)} all-gather(bf16[32,2048]{1,0:T(8,128)(2,1)S(1)} %multiply_convert_fusion), channel_id=1, replica_groups=mesh['dp'=8,'fsdp'=4] {'fsdp'}, dimensions={0}, use_global_device_ids=true | all-gather | bytes 655360 | tf_op jit(solution)/shard_map/all_gather | solution.py:138
  141.7 3.3 gather_fusion
  145.0 2.4 broadcast_in_dim.52
  147.4 92.2 %scatter_fusion = bf16[8,128,2048]{2,1,0:T(8,128)(2,1)} fusion(bf16[8,128,2048]{2,1,0:T(8,128)(2,1)} %broadcast_in_dim.52, s32[512]{0:T(512)S(1)} %bitcast.133, bf16[512,2048]{1,0:T(8,128)(2,1)} %gather_fusion), kind=kCustom, calls=%fused_computation.3 | custom fusion | bytes 6295552 | tf_op jit(solution)/shard_map/scatter | solution.py:151
  239.6 98.7 %all_to_all.10 = bf16[8,1,128,2048]{3,2,1,0:T(8,128)(2,1)S(1)} all-to-all(bf16[8,1,128,2048]{3,2,1,0:T(8,128)(2,1)} %bitcast.132), channel_id=1, replica_groups=mesh['dp'=8,'fsdp'=4] {'dp'}, dimensions={0} | all-to-all | bytes 8388608 | tf_op jit(solution)/shard_map/all_to_all | solution.py:156
  338.3 3.2 fusion.6
  341.5 4.4 convert_bitcast_fusion
  345.9 4.7 all-to-all-start.1
  351.2 2.6 gather_fusion.2
  354.1 89.4 %all-to-all-done.1 = bf16[8,1,128,2048]{3,2,1,0:T(8,128)(2,1)} async-done(((bf16[8,1,128,2048]{3,2,1,0:T(8,128)(2,1)}), bf16[8,1,128,2048]{3,2,1,0:T(8,128)(2,1)}, u32[]{:S(2)}, u32[]{:S(2)}) %all-to-all-start.1) | async-done | bytes 4194336 | tf_op jit(solution)/shard_map/all_to_all | solution.py:158
  443.5 8.0 %gather_fusion.1 = bf16[512,2048]{1,0:T(8,128)(2,1)} fusion(bf16[1024,2048]{1,0:T(8,128)(2,1)} %bitcast.34, s32[1024]{0:T(1024)S(1)} %pad_clamp_fusion), kind=kCustom, calls=%fused_computation.1 | custom fusion | bytes 4196352 | tf_op jit(solution)/shard_map/gather | solution.py:159
  451.5 4.9 reshape.626
  456.4 6.4 %multiply_reduce_fusion = f32[128,2048]{1,0:T(8,128)} fusion(f32[128,4,2048]{2,1,0:T(4,128)} %reshape.626, f32[128,4]{1,0:T(8,128)S(1)} %copy.102), kind=kLoop, calls=%fused_computation.7 | loop fusion | flops 1835008 | bytes 5244928 | tf_op jit(solution)/shard_map/reduce_sum | solution.py:160
  464.7 21.2 %reduce-scatter.2.cloned.1.call-done = f32[32,2048]{1,0:T(8,128)} async-done(((f32[128,2048]{1,0:T(8,128)}), f32[32,2048]{1,0:T(8,128)}) %reduce-scatter.2.cloned.1.call-update) | async-done | bytes 262160 | tf_op jit(solution)/shard_map/reduce_scatter | solution.py:163
  485.9 1.0 add_convert_fusion
  486.9 41.3 %all-gather = bf16[32,1,2048]{2,1,0:T(2,128)(2,1)S(1)} all-gather(bf16[1,1,2048]{2,1,0:T(2,128)(2,1)S(1)} %fusion.49), channel_id=1, replica_groups=mesh['dp'=8,'fsdp'=4] {'dp','fsdp'}, dimensions={0}, use_global_device_ids=true | all-gather | bytes 135168 | tf_op jit(solution)/shard_map/all_gather | solution.py:167
  528.2 1.5 scatter_custom_fusion.1
  (83 shorter events, 6.7 us)
Async XLA Ops:
  7.2 331.2 %copy-start = (bf16[1,2,2048,352]{2,3,1,0:T(8,128)(2,1)S(1)}, bf16[1,2,2048,352]{2,3,1,0:T(8,128)(2,1)}, u32[]{:S(2)}) copy-start(bf16[1,2,2048,352]{2,3,1,0:T(8,128)(2,1)} %param.28) | copy-start | bytes 8650756
  7.2 1.5 copy-start.10
  7.2 1.9 copy-start.14
  7.2 87.2 %all-gather.4.cloned.1.call-start = ((), (), s32[]{:S(2)}) async-start(), calls=%async_computation.3 | async-start | bytes 15728640 | tf_op jit(solution)/shard_map/all_gather | solution.py:120
  7.9 122.6 %all-gather.6.cloned.1.call-start = ((), (), s32[]{:S(2)}) async-start(), calls=%async_computation.4 | async-start | bytes 5242880 | tf_op jit(solution)/shard_map/all_gather | solution.py:134
  15.1 8.1 %copy-start.4 = (bf16[32,2048]{1,0:T(8,128)(2,1)S(1)}, bf16[32,2048]{1,0:T(8,128)(2,1)}, u32[]{:S(2)}) copy-start(bf16[32,2048]{1,0:T(8,128)(2,1)} %param.15) | copy-start | bytes 393220
  15.1 79.4 %copy-start.7 = (f32[2048]{0:T(1024)S(1)}, f32[2048]{0:T(1024)}, u32[]{:S(2)}) copy-start(f32[2048]{0:T(1024)} %param.21) | copy-start | bytes 24580
  15.1 79.4 %copy-start.11 = (f32[3072]{0:T(1024)S(1)}, f32[3072]{0:T(1024)}, u32[]{:S(2)}) copy-start(f32[3072]{0:T(1024)} %param.23) | copy-start | bytes 36868
  101.7 4.1 copy-start.5
  106.5 27.9 %copy-start.12 = (f32[2048]{0:T(1024)S(1)}, f32[2048]{0:T(1024)}, u32[]{:S(2)}) copy-start(f32[2048]{0:T(1024)} %param.25) | copy-start | bytes 24580
  133.6 0.7 copy-start.2
  338.3 3.2 copy-start.13
  345.9 5.0 copy-start.9
  345.9 97.5 %all-to-all-start.1 = ((bf16[8,1,128,2048]{3,2,1,0:T(8,128)(2,1)}), bf16[8,1,128,2048]{3,2,1,0:T(8,128)(2,1)}, u32[]{:S(2)}, u32[]{:S(2)}) async-start(bf16[8,1,128,2048]{3,2,1,0:T(8,128)(2,1)} %convert_bitcast_fusion), calls=%async_computation.1 | async-start | bytes 8388608 | tf_op jit(solution)/shard_map/all_to_all | solution.py:158
  350.6 135.3 %reduce-scatter.2.cloned.1.call-start = ((), (), s32[]{:S(2)}) async-start(), calls=%async_computation.5 | async-start | bytes 1310720 | tf_op jit(solution)/shard_map/reduce_scatter | solution.py:163
  451.5 78.3 %copy-start.1 = (bf16[1,2,2048,352]{2,3,1,0:T(8,128)(2,1)S(1)}, bf16[1,2,2048,352]{2,3,1,0:T(8,128)(2,1)}, u32[]{:S(2)}) copy-start(bf16[1,2,2048,352]{2,3,1,0:T(8,128)(2,1)} %param.28) | copy-start | bytes 8650756
  456.4 7.1 %copy-start.8 = (f32[32,32]{1,0:T(8,128)S(1)}, f32[32,32]{1,0:T(8,128)}, u32[]{:S(2)}) copy-start(f32[32,32]{1,0:T(8,128)} %get-tuple-element.37) | copy-start | bytes 12292
  456.4 7.2 %copy-start.15 = (s32[32]{0:T(128)S(1)}, s32[32]{0:T(128)}, u32[]{:S(2)}) copy-start(s32[32]{0:T(128)} %param.20) | copy-start | bytes 388
  456.4 29.5 %copy-start.3 = (f32[32,2048]{1,0:T(8,128)S(1)}, f32[32,2048]{1,0:T(8,128)}, u32[]{:S(2)}) copy-start(f32[32,2048]{1,0:T(8,128)} %copy-done.2) | copy-start | bytes 786436
  486.9 42.8 %copy-start.6 = (bf16[32,2048]{1,0:T(8,128)(2,1)}, bf16[32,2048]{1,0:T(8,128)(2,1)S(1)}, u32[]{:S(2)}) copy-start(bf16[32,2048]{1,0:T(8,128)(2,1)S(1)} %add_convert_fusion) | copy-start | bytes 393220
Sparse Core Ops, SparseCore 0:
  9.6 84.8 all-gather.3
  96.0 34.4 all-gather.5
  462.9 22.9 reduce-scatter.1
where the time goes:
time: 539 us; the launch traced here: 536 us
  waiting for transfers between devices  207 us (38%)
  blocking collectives  147 us (27%)
  local copies, waits for them, and re-layouts  128 us (24%)
  matrix products  23.4 us (4%)
  between operations  15.4 us (3%)
  other arithmetic  10.7 us (2%)
    all_to_all x1, blocking collectives, per_device(): lax.all_to_all(buffer, 'dp', split_axis=0, concat_axis=0, tiled=True)  98.7 us
    scatter x1, local copies, waits for them, and re-layouts, per_device(): buffer = jnp.zeros((experts, capacity, D), jnp.bfloat16).at[flat_expert,...  92.2 us
    all_to_all x1, waiting for transfers between devices, per_device(): lax.all_to_all(parts, 'dp', split_axis=0, concat_axis=0, tiled=True)  89.4 us
    all_gather x1, waiting for transfers between devices, per_device(): wide_qkv = lax.all_gather(w_qkv, 'fsdp', axis=1, tiled=True)  71.1 us
    all_gather x1, blocking collectives, per_device(): everyone = lax.all_gather(last_rows, ('dp', 'fsdp'), axis=0, tiled=True)  41.3 us
    all_gather x1, waiting for transfers between devices, per_device(): wide_out = lax.all_gather(w_out, 'fsdp', axis=1, tiled=True)  23.8 us
    reduce_scatter x1, waiting for transfers between devices, per_device(): moe = lax.psum_scatter(weighted, 'fsdp', scatter_dimension=0, tiled=True)  21.2 us
  transfers between devices with their start and end apart: 4, of which 4 were waited for; matrix products, arithmetic and copies ran while one was open for 6% of the time, Pallas kernels for 0%

commit v1 on v0

--- a/solution.py
+++ b/solution.py
@@ -81,9 +81,11 @@
 
 def slots_of(group_ids, experts):
     flat = group_ids.reshape(-1)
-    onehot = (flat[:, None] == jnp.arange(experts, dtype=jnp.int32)[None, :]).astype(jnp.int32)
-    earlier = jnp.cumsum(onehot, axis=0) - onehot
-    return jnp.sum(earlier * onehot, axis=1)
+    onehot = (flat[:, None] == jnp.arange(experts, dtype=jnp.int32)[None, :]).astype(jnp.bfloat16)
+    index = jnp.arange(flat.shape[0], dtype=jnp.int32)
+    before = (index[None, :] < index[:, None]).astype(jnp.bfloat16)
+    earlier = jnp.dot(before, onehot, preferred_element_type=jnp.float32)
+    return jnp.sum(earlier * onehot.astype(jnp.float32), axis=1).astype(jnp.int32)
 
 
 def expert_math(received, w_gate_up, w_down):
@@ -94,6 +96,62 @@
     return jnp.einsum("gecf,efd->gecd", hidden, w_down, preferred_element_type=jnp.float32).astype(
         jnp.bfloat16
     )
+
+
+def routed_experts(moe_input, router, expert_ids, w_gate_up, w_down):
+    group_input = lax.all_gather(moe_input, "fsdp", axis=0, tiled=True)
+    group_rows = group_input.shape[0]
+    experts = router.shape[1]
+    chosen_count = expert_ids.shape[1]
+    logits = jnp.dot(group_input, router, preferred_element_type=jnp.float32)
+    gates = jax.nn.sigmoid(jnp.take_along_axis(logits, expert_ids, axis=1))
+    slots = slots_of(expert_ids, experts)
+    capacity = 2 * group_rows * chosen_count // experts
+    place = expert_ids * capacity + slots.reshape(expert_ids.shape)
+    hits = place[:, :, None] == jnp.arange(experts * capacity, dtype=jnp.int32)
+    dispatch = jnp.any(hits, axis=1).astype(jnp.bfloat16)
+    buffer = jnp.einsum(
+        "ts,td->sd", dispatch, group_input, preferred_element_type=jnp.float32
+    ).astype(jnp.bfloat16)
+    local_experts = w_gate_up.shape[0]
+    buffer = buffer.reshape(experts // local_experts, local_experts, capacity, D)
+    parts = expert_math(
+        lax.all_to_all(buffer, "dp", split_axis=0, concat_axis=0, tiled=True), w_gate_up, w_down
+    )
+    returned = lax.all_to_all(parts, "dp", split_axis=0, concat_axis=0, tiled=True)
+    combine = jnp.sum(jnp.where(hits, gates[:, :, None], 0.0), axis=1)
+    weighted = jnp.dot(
+        combine,
+        returned.reshape(experts * capacity, D).astype(jnp.float32),
+        precision=lax.Precision.HIGHEST,
+    )
+    return lax.psum_scatter(weighted, "fsdp", scatter_dimension=0, tiled=True)
+
+
+def dense_experts(moe_input, router, expert_ids, w_gate_up, w_down):
+    rows = moe_input.shape[0]
+    experts = router.shape[1]
+    mine = lax.dynamic_slice_in_dim(expert_ids, lax.axis_index("fsdp") * rows, rows)
+    logits = jnp.dot(moe_input, router, preferred_element_type=jnp.float32)
+    chosen = jnp.any(mine[:, :, None] == jnp.arange(experts, dtype=jnp.int32), axis=1)
+    gates = jnp.where(chosen, jax.nn.sigmoid(logits), 0.0)
+    high = gates.astype(jnp.bfloat16)
+    low = (gates - high.astype(jnp.float32)).astype(jnp.bfloat16)
+    side = jnp.pad(jnp.concatenate([high, low], axis=1), ((0, 0), (0, 128 - 2 * experts)))
+    packed = jnp.concatenate([moe_input, side], axis=1)
+    everyone = lax.all_gather(packed, ("dp", "fsdp"), axis=0, tiled=True)
+    tokens = everyone[:, :D]
+    expert = lax.axis_index("dp")
+    side = everyone[:, D:].astype(jnp.float32)
+    lane = jnp.arange(128, dtype=jnp.int32)
+    picked = (lane == expert) | (lane == expert + experts)
+    gate = jnp.sum(jnp.where(picked[None, :], side, 0.0), axis=1, keepdims=True)
+    first = jnp.dot(tokens, w_gate_up[0, 0], preferred_element_type=jnp.float32)
+    second = jnp.dot(tokens, w_gate_up[0, 1], preferred_element_type=jnp.float32)
+    hidden = (jax.nn.silu(first) * second).astype(jnp.bfloat16)
+    part = jnp.dot(hidden, w_down[0], preferred_element_type=jnp.float32)
+    part = (part * gate).astype(jnp.bfloat16)
+    return lax.psum_scatter(part, ("dp", "fsdp"), scatter_dimension=0, tiled=True)
 
 
 def per_device(
@@ -116,10 +174,14 @@
     rows = drafts.shape[0]
     requests = cache.shape[0]
     feature = HEADS * HD
-    normed = scaled_norm(drafts, attn_gain)
-    wide_qkv = lax.all_gather(w_qkv, "fsdp", axis=1, tiled=True)
-    full_qkv = jnp.dot(normed, wide_qkv, preferred_element_type=jnp.float32)
-    qkv = (full_qkv + qkv_bias).astype(jnp.bfloat16).reshape(rows, HEADS, 3, HD)
+    group = lax.all_gather(drafts, "fsdp", axis=0, tiled=True)
+    w_out, group = lax.optimization_barrier((w_out, group))
+    normed = scaled_norm(group, attn_gain)
+    columns = w_qkv.shape[1]
+    mine = lax.axis_index("fsdp") * columns
+    bias = lax.dynamic_slice_in_dim(qkv_bias, mine, columns)
+    part_qkv = (jnp.dot(normed, w_qkv, preferred_element_type=jnp.float32) + bias).astype(jnp.bfloat16)
+    qkv = lax.all_to_all(part_qkv, "fsdp", split_axis=0, concat_axis=1, tiled=True)
     qkv = qkv.reshape(requests, TREE, HEADS, 3, HD)
 
     def per_request(block, cache_block, valid_slots, parent_row, accepted_node):
@@ -135,33 +197,11 @@
     projected = jnp.dot(attn, wide_out, preferred_element_type=jnp.float32)
     resid = (drafts.astype(jnp.float32) + projected).astype(jnp.bfloat16)
     moe_input = scaled_norm(resid, moe_gain)
-    group_input = lax.all_gather(moe_input, "fsdp", axis=0, tiled=True)
-    group_rows = group_input.shape[0]
-    experts = router.shape[1]
-    chosen_count = expert_ids.shape[1]
-    logits = jnp.dot(group_input, router, preferred_element_type=jnp.float32)
-    gates = jax.nn.sigmoid(jnp.take_along_axis(logits, expert_ids, axis=1))
-    slots = slots_of(expert_ids, experts)
-    capacity = 2 * group_rows * chosen_count // experts
-    flat_expert = expert_ids.reshape(-1)
-    token_index = jnp.arange(group_rows * chosen_count, dtype=jnp.int32) // chosen_count
-    buffer = (
-        jnp.zeros((experts, capacity, D), jnp.bfloat16)
-        .at[flat_expert, slots]
-        .set(group_input[token_index])
-    )
-    local_experts = w_gate_up.shape[0]
-    buffer = buffer.reshape(experts // local_experts, local_experts, capacity, D)
-    parts = expert_math(
-        lax.all_to_all(buffer, "dp", split_axis=0, concat_axis=0, tiled=True), w_gate_up, w_down
-    )
-    returned = lax.all_to_all(parts, "dp", split_axis=0, concat_axis=0, tiled=True)
-    picked = returned.reshape(experts * capacity, D)[flat_expert * capacity + slots]
-    weighted = jnp.sum(
-        picked.astype(jnp.float32).reshape(group_rows, chosen_count, D) * gates[:, :, None], axis=1
-    )
-    moe = lax.psum_scatter(weighted, "fsdp", scatter_dimension=0, tiled=True)
-    layer_out = (resid.astype(jnp.float32) + moe).astype(jnp.bfloat16)
+    if router.shape[1] <= 2 * expert_ids.shape[1] and w_gate_up.shape[0] == 1:
+        moe = dense_experts(moe_input, router, expert_ids, w_gate_up, w_down)
+    else:
+        moe = routed_experts(moe_input, router, expert_ids, w_gate_up, w_down)
+    layer_out = (resid.astype(jnp.float32) + moe.astype(jnp.float32)).astype(jnp.bfloat16)
     final_rows = layer_out.reshape(requests, TREE, D)
     last_rows = jnp.take_along_axis(final_rows, accepted[:, None, None], axis=1)[:, 0]
     everyone = lax.all_gather(last_rows, ("dp", "fsdp"), axis=0, tiled=True)

time: 539 us -> 328 us (0.61)
  local copies, waits for them, and re-layouts: 128 us -> 17.2 us
  blocking collectives: 147 us -> 47.5 us
    reduce_scatter x1, waiting for transfers between devices: 21.2 us -> 136 us  [dense_experts(): lax.psum_scatter(part, ('dp', 'fsdp'), scatter_dimension=0, tiled=True)]
    all_to_all x1 -> x0, blocking collectives: 98.7 us -> none  [per_device(): lax.all_to_all(buffer, 'dp', split_axis=0, concat_axis=0, tiled=True)]
    scatter x1 -> x0, local copies, waits for them, and re-layouts: 92.2 us -> none  [per_device(): buffer = jnp.zeros((experts, capacity, D), jnp.bfloat16).at[flat_expert,...]
    all_to_all x1, waiting for transfers between devices: 89.4 us -> 0.01 us  [per_device(): lax.all_to_all(part_qkv, 'fsdp', split_axis=0, concat_axis=1, tiled=True)]
    gather x7 -> x0, local copies, waits for them, and re-layouts: 14.3 us -> none  [the longest x1 8 us: per_device(): returned.reshape(experts * capacity, D)[flat_expert * capacity + slots]]
    all_gather x1, waiting for transfers between devices: 23.8 us -> 10.3 us  [per_device(): wide_out = lax.all_gather(w_out, 'fsdp', axis=1, tiled=True)]
    all_gather x1, waiting for transfers between devices: 71.1 us -> 63.1 us  [dense_experts(): everyone = lax.all_gather(packed, ('dp', 'fsdp'), axis=0, tiled=True)]
  transfers between devices with their start and end apart: 4 -> 4, of which waited for: 4 -> 3; matrix products, arithmetic and copies ran while one was open for 6% -> 8% of each run, Pallas kernels for 0% -> 0%
where the time goes in v1:
time: 328 us
  waiting for transfers between devices  209 us (64%)
  blocking collectives  47.5 us (14%)
  matrix products  25.4 us (8%)
  local copies, waits for them, and re-layouts  17.2 us (5%)
  between operations  15.3 us (5%)
  other arithmetic  9.66 us (3%)
  starting transfers between devices  3.49 us (1%)
    reduce_scatter x1, waiting for transfers between devices, dense_experts(): lax.psum_scatter(part, ('dp', 'fsdp'), scatter_dimension=0, tiled=True)  136 us
    all_gather x1, waiting for transfers between devices, dense_experts(): everyone = lax.all_gather(packed, ('dp', 'fsdp'), axis=0, tiled=True)  63.1 us
    all_gather x1, blocking collectives, per_device(): everyone = lax.all_gather(last_rows, ('dp', 'fsdp'), axis=0, tiled=True)  37 us
    all_gather x1, blocking collectives, per_device(): group = lax.all_gather(drafts, 'fsdp', axis=0, tiled=True)  10.4 us
    all_gather x1, waiting for transfers between devices, per_device(): wide_out = lax.all_gather(w_out, 'fsdp', axis=1, tiled=True)  10.3 us
    dot_general x1, matrix products, dense_experts(): part = jnp.dot(hidden, w_down[0], preferred_element_type=jnp.float32)  9.4 us
    unnamed x19, local copies, waits for them, and re-layouts  6.65 us
  transfers between devices with their start and end apart: 4, of which 3 were waited for; matrix products, arithmetic and copies ran while one was open for 8% of the time, Pallas kernels for 0%

profile of v1, /device:TPU:0, one launch (start us, length us, event | category | flops | bytes accessed | tf_op | source)
XLA Modules:
  0.0 327.6 jit_solution(10923147408537067673)
XLA Ops:
  7.2 10.4 %all_gather.12 = bf16[128,2048]{1,0:T(8,128)(2,1)} all-gather(bf16[32,2048]{1,0:T(8,128)(2,1)} %param.15), channel_id=1, replica_groups=mesh['dp'=8,'fsdp'=4] {'fsdp'}, dimensions={0}, use_global_device_ids=true | all-gather | bytes 655360 | tf_op jit(solution)/shard_map/all_gather | solution.py:177
  17.7 0.8 dynamic_slice.6
  18.4 1.2 fusion.30
  19.7 2.4 fusion.20
  22.1 3.4 %all-to-all-start = ((bf16[4,32,768]{2,1,0:T(8,128)(2,1)}), bf16[4,32,768]{2,1,0:T(8,128)(2,1)S(1)}, u32[]{:S(2)}, u32[]{:S(2)}) async-start(bf16[4,32,768]{2,1,0:T(8,128)(2,1)} %bitcast.1), calls=%async_computation | async-start | bytes 393216 | tf_op jit(solution)/shard_map/all_to_all | solution.py:184
  27.0 4.1 %fusion.77 = (bf16[1,1,768,1024]{3,2,1,0:T(8,128)(2,1)}, bf16[1,1,768,1024]{3,2,1,0:T(8,128)(2,1)}) fusion(bf16[1,2,768,1024]{3,2,1,0:T(8,128)(2,1)} %param.16), kind=kLoop, calls=%fused_computation.115 | loop fusion | bytes 6291456 | tf_op jit(solution)/shard_map/vmap()/slice | solution.py:38
  31.2 2.6 copy.101
  33.8 2.6 copy.103
  37.0 0.8 copy.82
  37.9 1.0 reshape.393
  38.9 1.6 slice_reduce_fusion.1
  40.7 1.8 fusion.78
  42.9 0.7 convolution_bitcast_fusion
  43.8 0.7 copy.92
  44.4 10.3 %all-gather.4.cloned.1.call-done = bf16[1024,2048]{1,0:T(8,128)(2,1)} async-done(((bf16[1024,512]{1,0:T(8,128)(2,1)}), bf16[1024,2048]{1,0:T(8,128)(2,1)}) %all-gather.4.cloned.1.call-update) | async-done | bytes 4194320 | tf_op jit(solution)/shard_map/all_gather | solution.py:196
  54.8 3.2 multiply_reduce_fusion
  58.0 0.8 multiply_convert_fusion.1
  58.8 0.9 subtract_convert_fusion
  60.3 1.4 copy.105
  61.6 1.4 fusion.45
  63.1 63.1 %all-gather.6.cloned.1.call-done = bf16[1024,2176]{1,0:T(8,128)(2,1)} async-done(((bf16[32,2176]{1,0:T(8,128)(2,1)}), bf16[1024,2176]{1,0:T(8,128)(2,1)}) %all-gather.6.cloned.1.call-update) | async-done | bytes 4456464 | tf_op jit(solution)/shard_map/all_gather | solution.py:142
  126.2 1.1 select_reduce_fusion
  127.3 5.5 %fusion.2 = f32[1024,352]{0,1:T(8,128)} fusion(bf16[1024,2176]{1,0:T(8,128)(2,1)} %all-gather.6.cloned.1.call-done, bf16[1,2,2048,352]{2,3,1,0:T(8,128)(2,1)} %param.28), kind=kOutput, calls=%fused_computation.4 | convolution fusion | flops 1476395008 | bytes 7077888 | tf_op jit(solution)/shard_map/dot_general | solution.py:149
  132.8 9.4 %multiply_convert_fusion = bf16[1024,2048]{1,0:T(8,128)(2,1)} fusion(f32[1024]{0:T(1024)S(1)} %select_reduce_fusion, bf16[1,352,2048]{2,1,0:T(8,128)(2,1)} %param.29, bf16[1,2,2048,352]{2,3,1,0:T(8,128)(2,1)} %param.28, bf16[1024,2176]{1,0:T(8,128)(2,1)} %all-gather.6.cloned.1.call-done, f32[1024,352]{0,1:T(8,128)} %fusion.2), kind=kOutput, calls=%fused_computation.1 | convolution fusion | flops 2959147008 | bytes 12718080 | tf_op jit(solution)/shard_map/dot_general | solution.py:152
  142.9 0.7 reduce_sum.59
  143.6 0.7 compare_select_fusion
  144.3 0.7 broadcast_add_fusion
  145.3 0.7 maximum_bitcast_fusion
  146.0 135.5 %reduce-scatter.2.cloned.1.call-done = bf16[32,2048]{1,0:T(8,128)(2,1)} async-done(((bf16[1024,2048]{1,0:T(8,128)(2,1)}), bf16[32,2048]{1,0:T(8,128)(2,1)}) %reduce-scatter.2.cloned.1.call-update) | async-done | bytes 131088 | tf_op jit(solution)/shard_map/reduce_scatter | solution.py:154
  281.5 0.9 add_convert_fusion
  282.5 37.0 %all-gather = bf16[32,1,2048]{2,1,0:T(2,128)(2,1)S(1)} all-gather(bf16[1,1,2048]{2,1,0:T(2,128)(2,1)S(1)} %fusion.63), channel_id=1, replica_groups=mesh['dp'=8,'fsdp'=4] {'dp','fsdp'}, dimensions={0}, use_global_device_ids=true | all-gather | bytes 135168 | tf_op jit(solution)/shard_map/all_gather | solution.py:207
  319.6 1.5 scatter_custom_fusion
  (47 shorter events, 3.6 us)
Async XLA Ops:
  7.2 12.5 %copy-start = (bf16[2048,768]{1,0:T(8,128)(2,1)S(1)}, bf16[2048,768]{1,0:T(8,128)(2,1)}, u32[]{:S(2)}) copy-start(bf16[2048,768]{1,0:T(8,128)(2,1)} %param.22) | copy-start | bytes 9437188
  7.2 47.6 %all-gather.4.cloned.1.call-start = ((), (), s32[]{:S(2)}) async-start(), calls=%async_computation.2 | async-start | bytes 5242880 | tf_op jit(solution)/shard_map/all_gather | solution.py:196
  17.6 8.5 %copy-start.6 = (s32[128,4]{0,1:T(4,128)S(1)}, s32[128,4]{0,1:T(4,128)}, u32[]{:S(2)}) copy-start(s32[128,4]{0,1:T(4,128)} %param.27) | copy-start | bytes 6148
  17.6 8.6 %copy-start.7 = (s32[1,32]{1,0:T(1,128)S(1)}, s32[1,32]{1,0:T(1,128)}, u32[]{:S(2)}) copy-start(s32[1,32]{1,0:T(1,128)} %param.18) | copy-start | bytes 388
  22.1 15.0 %all-to-all-start = ((bf16[4,32,768]{2,1,0:T(8,128)(2,1)}), bf16[4,32,768]{2,1,0:T(8,128)(2,1)S(1)}, u32[]{:S(2)}, u32[]{:S(2)}) async-start(bf16[4,32,768]{2,1,0:T(8,128)(2,1)} %bitcast.1), calls=%async_computation | async-start | bytes 393216 | tf_op jit(solution)/shard_map/all_to_all | solution.py:184
  25.4 100.8 %all-gather.6.cloned.1.call-start = ((), (), s32[]{:S(2)}) async-start(), calls=%async_computation.3 | async-start | bytes 4595712 | tf_op jit(solution)/shard_map/all_gather | solution.py:142
  38.9 4.0 %copy-start.1 = (bf16[1,1,768,1024]{2,3,1,0:T(8,128)(2,1)S(1)}, bf16[1,1,768,1024]{2,3,1,0:T(8,128)(2,1)}, u32[]{:S(2)}) copy-start(bf16[1,1,768,1024]{2,3,1,0:T(8,128)(2,1)} %copy.103) | copy-start | bytes 4718596
  42.6 12.2 %copy-start.2 = (bf16[32,2048]{1,0:T(8,128)(2,1)S(1)}, bf16[32,2048]{1,0:T(8,128)(2,1)}, u32[]{:S(2)}) copy-start(bf16[32,2048]{1,0:T(8,128)(2,1)} %param.15) | copy-start | bytes 393220
  63.0 218.5 %reduce-scatter.2.cloned.1.call-start = ((), (), s32[]{:S(2)}) async-start(), calls=%async_computation.4 | async-start | bytes 4325376 | tf_op jit(solution)/shard_map/reduce_scatter | solution.py:154
  142.2 2.7 copy-start.4
  142.2 2.9 copy-start.3
  282.5 38.6 %copy-start.5 = (bf16[32,2048]{1,0:T(8,128)(2,1)}, bf16[32,2048]{1,0:T(8,128)(2,1)S(1)}, u32[]{:S(2)}) copy-start(bf16[32,2048]{1,0:T(8,128)(2,1)S(1)} %add_convert_fusion) | copy-start | bytes 393220
Sparse Core Ops, SparseCore 0:
  17.8 36.9 all-gather.3
  63.2 63.0 all-gather.5
  142.3 139.1 reduce-scatter.1

commit v2 on v1

--- a/solution.py
+++ b/solution.py
@@ -1,8 +1,11 @@
+import functools
 import math
 
 import jax
 import jax.numpy as jnp
 from jax import lax
+from jax.experimental import pallas as pl
+from jax.experimental.pallas import tpu as pltpu
 from jax.sharding import PartitionSpec as P
 
 D = 2048
@@ -128,6 +131,136 @@
     return lax.psum_scatter(weighted, "fsdp", scatter_dimension=0, tiled=True)
 
 
+CORE, X, Y, ZHI, ZLO = range(5)
+
+
+def my_bits():
+    d, f = lax.axis_index("dp"), lax.axis_index("fsdp")
+    return (f % 2, f // 2, d % 2, d // 4, (d // 2) % 2)
+
+
+def partner(axis):
+    d, f = lax.axis_index("dp"), lax.axis_index("fsdp")
+    bit = my_bits()[axis]
+    step = {CORE: 1, X: 2, Y: 1, ZHI: 4, ZLO: 2}[axis]
+    other = step - 2 * step * bit
+    return (d, f + other) if axis in (CORE, X) else (d + other, f)
+
+
+def meet_partners():
+    barrier = pltpu.get_barrier_semaphore()
+    for axis in range(5):
+        pl.semaphore_signal(
+            barrier, inc=1, device_id=partner(axis), device_id_type=pl.DeviceIdType.MESH
+        )
+    pl.semaphore_wait(barrier, 5)
+
+
+def gather_kernel(orders, columns, in_ref, out_ref, send_sem, recv_sem):
+    bits = my_bits()
+    out_ref[bits] = in_ref[...]
+    meet_partners()
+    for step in range(5):
+        copies = []
+        for p, order in enumerate(orders):
+            done = order[:step]
+            where = tuple(pl.ds(0, 2) if a in done else bits[a] for a in range(5))
+            where = where + (slice(None), pl.ds(*columns[p]))
+            copies.append(
+                pltpu.make_async_remote_copy(
+                    src_ref=out_ref.at[where],
+                    dst_ref=out_ref.at[where],
+                    send_sem=send_sem.at[p, step],
+                    recv_sem=recv_sem.at[p, step],
+                    device_id=partner(order[step]),
+                    device_id_type=pl.DeviceIdType.MESH,
+                )
+            )
+            copies[-1].start()
+        for copy in copies:
+            copy.wait()
+
+
+def gather_blocks(block, orders, columns, number):
+    shape = (2,) * 5 + block.shape
+    return pl.pallas_call(
+        functools.partial(gather_kernel, orders, columns),
+        out_shape=jax.ShapeDtypeStruct(shape, block.dtype),
+        in_specs=[pl.BlockSpec(memory_space=pltpu.VMEM)],
+        out_specs=pl.BlockSpec(memory_space=pltpu.VMEM),
+        scratch_shapes=[
+            pltpu.SemaphoreType.DMA((len(orders), 5)),
+            pltpu.SemaphoreType.DMA((len(orders), 5)),
+        ],
+        compiler_params=pltpu.CompilerParams(
+            collective_id=number, has_side_effects=True, vmem_limit_bytes=40 * 1024 * 1024
+        ),
+    )(block)
+
+
+def scatter_kernel(orders, columns, in_ref, out_ref, r0, r1, r2, r3, r4, send_sem, recv_sem):
+    bits = my_bits()
+    received = (r0, r1, r2, r3, r4)
+    meet_partners()
+    for step in range(5):
+        copies = []
+        held = in_ref if step == 0 else received[step - 1]
+        for p, order in enumerate(orders):
+            left = [a for a in range(5) if a not in order[:step]]
+            give = tuple(1 - bits[a] if a == order[step] else pl.ds(0, 2) for a in left)
+            tail = (slice(None), pl.ds(*columns[p]))
+            into = tuple(pl.ds(0, 2) for _ in left[1:])
+            copies.append(
+                pltpu.make_async_remote_copy(
+                    src_ref=held.at[give + tail],
+                    dst_ref=received[step].at[into + tail],
+                    send_sem=send_sem.at[p, step],
+                    recv_sem=recv_sem.at[p, step],
+                    device_id=partner(order[step]),
+                    device_id_type=pl.DeviceIdType.MESH,
+                )
+            )
+            copies[-1].start()
+        for p, order in enumerate(orders):
+            copies[p].wait()
+            left = [a for a in range(5) if a not in order[:step]]
+            spot = left.index(order[step])
+            count = len(left) - 1
+            tail = (slice(None), pl.ds(*columns[p]))
+
+            def add(i, carry):
+                index = tuple((i // 2 ** (count - 1 - k)) % 2 for k in range(count))
+                mine = index[:spot] + (bits[order[step]],) + index[spot:]
+                total = held[mine + tail].astype(jnp.float32) + received[step][
+                    index + tail
+                ].astype(jnp.float32)
+                received[step][index + tail] = total.astype(jnp.bfloat16)
+                return carry
+
+            lax.fori_loop(0, 2**count, add, 0)
+    out_ref[...] = received[4][...]
+
+
+def scatter_sum(blocks, orders, columns, number):
+    rows, width = blocks.shape[5:]
+    return pl.pallas_call(
+        functools.partial(scatter_kernel, orders, columns),
+        out_shape=jax.ShapeDtypeStruct((rows, width), blocks.dtype),
+        in_specs=[pl.BlockSpec(memory_space=pltpu.VMEM)],
+        out_specs=pl.BlockSpec(memory_space=pltpu.VMEM),
+        scratch_shapes=[
+            pltpu.VMEM((2,) * (4 - step) + (rows, width), jnp.bfloat16) for step in range(5)
+        ]
+        + [
+            pltpu.SemaphoreType.DMA((len(orders), 5)),
+            pltpu.SemaphoreType.DMA((len(orders), 5)),
+        ],
+        compiler_params=pltpu.CompilerParams(
+            collective_id=number, has_side_effects=True, vmem_limit_bytes=40 * 1024 * 1024
+        ),
+    )(blocks)
+
+
 def dense_experts(moe_input, router, expert_ids, w_gate_up, w_down):
     rows = moe_input.shape[0]
     experts = router.shape[1]
@@ -139,7 +272,9 @@
     low = (gates - high.astype(jnp.float32)).astype(jnp.bfloat16)
     side = jnp.pad(jnp.concatenate([high, low], axis=1), ((0, 0), (0, 128 - 2 * experts)))
     packed = jnp.concatenate([moe_input, side], axis=1)
-    everyone = lax.all_gather(packed, ("dp", "fsdp"), axis=0, tiled=True)
+    orders = ((ZLO, ZHI, Y, X, CORE), (ZLO, ZHI, X, Y, CORE))
+    everyone = gather_blocks(packed, orders, ((0, D // 2), (D // 2, D // 2 + 128)), 1)
+    everyone = everyone.reshape(-1, D + 128)
     tokens = everyone[:, :D]
     expert = lax.axis_index("dp")
     side = everyone[:, D:].astype(jnp.float32)
@@ -151,7 +286,9 @@
     hidden = (jax.nn.silu(first) * second).astype(jnp.bfloat16)
     part = jnp.dot(hidden, w_down[0], preferred_element_type=jnp.float32)
     part = (part * gate).astype(jnp.bfloat16)
-    return lax.psum_scatter(part, ("dp", "fsdp"), scatter_dimension=0, tiled=True)
+    orders = ((CORE, X, Y, ZHI, ZLO), (CORE, Y, X, ZHI, ZLO))
+    blocks = part.reshape((2,) * 5 + (rows, D))
+    return scatter_sum(blocks, orders, ((0, D // 2), (D // 2, D // 2)), 2)
 
 
 def per_device(
@@ -197,14 +334,21 @@
     projected = jnp.dot(attn, wide_out, preferred_element_type=jnp.float32)
     resid = (drafts.astype(jnp.float32) + projected).astype(jnp.bfloat16)
     moe_input = scaled_norm(resid, moe_gain)
-    if router.shape[1] <= 2 * expert_ids.shape[1] and w_gate_up.shape[0] == 1:
+    small = (lax.axis_size("dp"), lax.axis_size("fsdp")) == (8, 4)
+    small = small and router.shape[1] <= 2 * expert_ids.shape[1] and w_gate_up.shape[0] == 1
+    if small and requests == 1:
         moe = dense_experts(moe_input, router, expert_ids, w_gate_up, w_down)
     else:
         moe = routed_experts(moe_input, router, expert_ids, w_gate_up, w_down)
     layer_out = (resid.astype(jnp.float32) + moe.astype(jnp.float32)).astype(jnp.bfloat16)
     final_rows = layer_out.reshape(requests, TREE, D)
     last_rows = jnp.take_along_axis(final_rows, accepted[:, None, None], axis=1)[:, 0]
-    everyone = lax.all_gather(last_rows, ("dp", "fsdp"), axis=0, tiled=True)
+    if small and requests == 1:
+        row = last_rows.reshape(D // 128, 128)
+        everyone = gather_blocks(row, ((CORE, X, Y, ZLO, ZHI),), ((0, 128),), 3)
+        everyone = everyone.transpose(3, 4, 2, 1, 0, 5, 6).reshape(-1, D)
+    else:
+        everyone = lax.all_gather(last_rows, ("dp", "fsdp"), axis=0, tiled=True)
     last_state = jnp.zeros_like(everyone).at[order].set(everyone)
     return (layer_out, appended, last_state)
 

time: 328 us -> 192 us (0.59)
  waiting for transfers between devices: 209 us -> 7.59 us
  Pallas kernels: 0 us -> 107 us
  blocking collectives: 47.5 us -> 10.4 us
  other arithmetic: 9.66 us -> 4.37 us
    reduce_scatter x1 -> x0, waiting for transfers between devices: 136 us -> none  [dense_experts(): lax.psum_scatter(part, ('dp', 'fsdp'), scatter_dimension=0, tiled=True)]
    pallas_call x0 -> x3, Pallas kernels: none -> 107 us  [the longest x2 64.1 us: gather_blocks(): pl.pallas_call(functools.partial(gather_kernel, orders, columns), out_sha...]
    all_gather x1 -> x0, waiting for transfers between devices: 63.1 us -> none  [dense_experts(): everyone = lax.all_gather(packed, ('dp', 'fsdp'), axis=0, tiled=True)]
    all_gather x1 -> x0, blocking collectives: 37 us -> none  [per_device(): everyone = lax.all_gather(last_rows, ('dp', 'fsdp'), axis=0, tiled=True)]
    unnamed x19 -> x30, local copies, waits for them, and re-layouts: 6.65 us -> 9.39 us
  transfers between devices with their start and end apart: 4 -> 2, of which waited for: 3 -> 1; matrix products, arithmetic and copies ran while one was open for 8% -> 13% of each run, Pallas kernels for 0% -> 0%
where the time goes in v2:
time: 192 us; the launch traced here: 191 us
  Pallas kernels  107 us (56%)
  matrix products  23 us (12%)
  local copies, waits for them, and re-layouts  19.8 us (10%)
  between operations  15.7 us (8%)
  blocking collectives  10.4 us (5%)
  waiting for transfers between devices  7.59 us (4%)
  other arithmetic  4.37 us (2%)
  starting transfers between devices  3.41 us (2%)
    pallas_call x2, Pallas kernels, gather_blocks(): pl.pallas_call(functools.partial(gather_kernel, orders, columns), out_sha...  64.1 us
    pallas_call x1, Pallas kernels, scatter_sum(): pl.pallas_call(functools.partial(scatter_kernel, orders, columns), out_sh...  42.7 us
    all_gather x1, blocking collectives, per_device(): group = lax.all_gather(drafts, 'fsdp', axis=0, tiled=True)  10.4 us
    dot_general x1, matrix products, dense_experts(): part = jnp.dot(hidden, w_down[0], preferred_element_type=jnp.float32)  9.4 us
    unnamed x30, local copies, waits for them, and re-layouts  9.39 us
    all_gather x1, waiting for transfers between devices, per_device(): wide_out = lax.all_gather(w_out, 'fsdp', axis=1, tiled=True)  7.57 us
    slice x1, local copies, waits for them, and re-layouts, attend(): cache_keys = cache_block[0].reshape(slots, HEADS, HD)  3.89 us
  transfers between devices with their start and end apart: 2, of which 1 were waited for; matrix products, arithmetic and copies ran while one was open for 13% of the time, Pallas kernels for 0%

profile of v2, /device:TPU:0, one launch (start us, length us, event | category | flops | bytes accessed | tf_op | source)
XLA Modules:
  0.0 191.1 jit_solution(2253944853408100468)
XLA Ops:
  7.2 10.4 %all_gather.6 = bf16[128,2048]{1,0:T(8,128)(2,1)} all-gather(bf16[32,2048]{1,0:T(8,128)(2,1)} %param.15), channel_id=1, replica_groups=mesh['dp'=8,'fsdp'=4] {'fsdp'}, dimensions={0}, use_global_device_ids=true | all-gather | bytes 655360 | tf_op jit(solution)/shard_map/all_gather | solution.py:314
  17.7 0.8 dynamic_slice.6
  18.5 1.2 fusion.30
  19.7 2.4 %fusion.20 = bf16[128,768]{1,0:T(8,128)(2,1)} fusion(bf16[2048,768]{1,0:T(8,128)(2,1)S(1)} %copy-done, bf16[128,2048]{1,0:T(8,128)(2,1)} %all_gather.6, f32[2048]{0:T(1024)} %param.21, f32[128]{0:T(128)S(1)} %add_rsqrt_fusion.1, f32[768]{0:T(1024)S(1)} %dynamic_slice.6), kind=kOutput, calls=%fused_computation.21 | convolution fusion | flops 403898368 | bytes 3878400 | tf_op jit(solution)/shard_map/dot_general | solution.py:320
  22.1 3.4 %all-to-all-start = ((bf16[4,32,768]{2,1,0:T(8,128)(2,1)}), bf16[4,32,768]{2,1,0:T(8,128)(2,1)S(1)}, u32[]{:S(2)}, u32[]{:S(2)}) async-start(bf16[4,32,768]{2,1,0:T(8,128)(2,1)} %bitcast.1), calls=%async_computation | async-start | bytes 393216 | tf_op jit(solution)/shard_map/all_to_all | solution.py:321
  27.0 0.5 compare_or_fusion
  27.7 0.5 compare_select_fusion
  28.1 0.6 broadcast_add_fusion
  28.7 3.9 %fusion.78 = (bf16[1,1,768,1024]{3,2,1,0:T(8,128)(2,1)}, bf16[1,1,768,1024]{3,2,1,0:T(8,128)(2,1)}) fusion(bf16[1,2,768,1024]{3,2,1,0:T(8,128)(2,1)} %param.16), kind=kLoop, calls=%fused_computation.116 | loop fusion | bytes 6291456 | tf_op jit(solution)/shard_map/vmap()/slice | solution.py:41
  32.6 0.5 fusion.74
  34.0 2.6 %copy.91 = bf16[1,1,768,1024]{2,3,1,0:T(8,128)(2,1)} copy(bf16[1,1,768,1024]{3,2,1,0:T(8,128)(2,1)} %get-tuple-element.33) | data formatting | bytes 3145728
  36.6 2.6 %copy.93 = bf16[1,1,768,1024]{2,3,1,0:T(8,128)(2,1)} copy(bf16[1,1,768,1024]{3,2,1,0:T(8,128)(2,1)} %get-tuple-element.34) | data formatting | bytes 3145728
  39.3 0.8 copy.70
  40.1 1.0 reshape.393
  41.1 0.9 slice_reduce_fusion.1
  42.3 1.9 fusion.79
  44.2 0.3 fusion.38
  44.5 0.7 convolution_bitcast_fusion
  45.2 0.2 fusion.23
  45.4 0.7 copy.80
  46.5 0.7 maximum_bitcast_fusion
  47.2 7.6 %all-gather.2.cloned.1.call-done = bf16[1024,2048]{1,0:T(8,128)(2,1)} async-done(((bf16[1024,512]{1,0:T(8,128)(2,1)}), bf16[1024,2048]{1,0:T(8,128)(2,1)}) %all-gather.2.cloned.1.call-update) | async-done | bytes 4194320 | tf_op jit(solution)/shard_map/all_gather | solution.py:333
  54.8 3.2 %multiply_reduce_fusion = (f32[32]{0:T(128)S(1)}, f32[32,2048]{1,0:T(8,128)S(1)}) fusion(bf16[1024,2048]{1,0:T(8,128)(2,1)} %all-gather.2.cloned.1.call-done, bf16[4,8,8,128]{3,2,1,0:T(8,128)(2,1)} %bitcast.109, bf16[32,2048]{1,0:T(8,128)(2,1)S(1)} %copy-done.4), kind=kOutput, calls=%fused_computation.56 | convolution fusion | flops 134610912 | bytes 4653184 | tf_op jit(solution)/shard_map/dot_general | solution.py:334
  58.1 1.1 subtract_convert_fusion
  59.3 47.8 %shard_map.169 = bf16[2,2,2,2,2,32,2176]{6,5,4,3,2,1,0:T(8,128)(2,1)S(1)} custom-call(bf16[32,2176]{1,0:T(8,128)(2,1)S(1)} %pad_maximum_fusion.in_ref), custom_call_target="tpu_custom_call" | custom-call | tf_op jit(solution)/shard_map/pallas_call | solution.py:186
  107.2 1.9 copy-done.1
  109.1 2.9 %fusion.2 = f32[1024,352]{0,1:T(8,128)} fusion(bf16[1024,2176]{1,0:T(8,128)(2,1)S(1)} %bitcast.100, bf16[1,2,2048,352]{2,3,1,0:T(8,128)(2,1)S(1)} %copy-done.11), kind=kOutput, calls=%fused_computation.4 | convolution fusion | flops 1476395008 | bytes 7077888 | tf_op jit(solution)/shard_map/dot_general | solution.py:284
  111.9 9.4 %multiply_convert_fusion = bf16[1024,2048]{1,0:T(8,128)(2,1)} fusion(f32[1024]{0:T(1024)S(1)} %select_reduce_fusion, bf16[1,352,2048]{2,1,0:T(8,128)(2,1)} %param.29, bf16[1,2,2048,352]{2,3,1,0:T(8,128)(2,1)} %param.28, bf16[1024,2176]{1,0:T(8,128)(2,1)} %bitcast.101, f32[1024,352]{0,1:T(8,128)} %fusion.2), kind=kOutput, calls=%fused_computation.1 | convolution fusion | flops 2959147008 | bytes 12718080 | tf_op jit(solution)/shard_map/dot_general | solution.py:287
  121.3 2.2 %copy-done.2 = bf16[1024,2048]{1,0:T(8,128)(2,1)S(1)} copy-done((bf16[1024,2048]{1,0:T(8,128)(2,1)S(1)}, bf16[1024,2048]{1,0:T(8,128)(2,1)}, u32[]{:S(2)}) %copy-start.2) | copy-done | bytes 4194328
  123.5 42.7 %shard_map.170 = bf16[32,2048]{1,0:T(8,128)(2,1)S(1)} custom-call(bf16[2,2,2,2,2,32,2048]{6,5,4,3,2,1,0:T(8,128)(2,1)S(1)} %bitcast.102), custom_call_target="tpu_custom_call" | custom-call | tf_op jit(solution)/shard_map/pallas_call | solution.py:246
  166.4 16.3 %shard_map.171 = bf16[2,2,2,2,2,16,128]{6,5,4,3,2,1,0:T(8,128)(2,1)S(1)} custom-call(bf16[16,128]{1,0:T(8,128)(2,1)S(1)} %bitcast.104), custom_call_target="tpu_custom_call" | custom-call | tf_op jit(solution)/shard_map/pallas_call | solution.py:186
  182.7 1.5 scatter_custom_fusion
  (56 shorter events, 2.3 us)
Async XLA Ops:
  7.2 12.5 %copy-start = (bf16[2048,768]{1,0:T(8,128)(2,1)S(1)}, bf16[2048,768]{1,0:T(8,128)(2,1)}, u32[]{:S(2)}) copy-start(bf16[2048,768]{1,0:T(8,128)(2,1)} %param.22) | copy-start | bytes 9437188
  7.2 47.6 %all-gather.2.cloned.1.call-start = ((), (), s32[]{:S(2)}) async-start(), calls=%async_computation.1 | async-start | bytes 5242880 | tf_op jit(solution)/shard_map/all_gather | solution.py:333
  17.6 8.5 %copy-start.12 = (s32[1,32]{1,0:T(1,128)S(1)}, s32[1,32]{1,0:T(1,128)}, u32[]{:S(2)}) copy-start(s32[1,32]{1,0:T(1,128)} %param.18) | copy-start | bytes 388
  17.6 9.9 %copy-start.9 = (s32[128,4]{0,1:T(4,128)S(1)}, s32[128,4]{0,1:T(4,128)}, u32[]{:S(2)}) copy-start(s32[128,4]{0,1:T(4,128)} %param.27) | copy-start | bytes 6148
  17.6 10.0 %copy-start.13 = (s32[32]{0:T(128)S(1)}, s32[32]{0:T(128)}, u32[]{:S(2)}) copy-start(s32[32]{0:T(128)} %param.20) | copy-start | bytes 388
  22.1 17.2 %all-to-all-start = ((bf16[4,32,768]{2,1,0:T(8,128)(2,1)}), bf16[4,32,768]{2,1,0:T(8,128)(2,1)S(1)}, u32[]{:S(2)}, u32[]{:S(2)}) async-start(bf16[4,32,768]{2,1,0:T(8,128)(2,1)} %bitcast.1), calls=%async_computation | async-start | bytes 393216 | tf_op jit(solution)/shard_map/all_to_all | solution.py:321
  41.1 3.4 %copy-start.3 = (bf16[1,1,768,1024]{2,3,1,0:T(8,128)(2,1)S(1)}, bf16[1,1,768,1024]{2,3,1,0:T(8,128)(2,1)}, u32[]{:S(2)}) copy-start(bf16[1,1,768,1024]{2,3,1,0:T(8,128)(2,1)} %copy.93) | copy-start | bytes 4718596
  44.2 1.9 copy-start.7
  44.2 1.9 copy-start.8
  44.5 10.3 %copy-start.4 = (bf16[32,2048]{1,0:T(8,128)(2,1)S(1)}, bf16[32,2048]{1,0:T(8,128)(2,1)}, u32[]{:S(2)}) copy-start(bf16[32,2048]{1,0:T(8,128)(2,1)} %param.15) | copy-start | bytes 393220
  45.2 12.8 %copy-start.6 = (f32[2048]{0:T(1024)S(1)}, f32[2048]{0:T(1024)}, u32[]{:S(2)}) copy-start(f32[2048]{0:T(1024)} %param.25) | copy-start | bytes 24580
  57.9 49.1 %copy-start.10 = (pred[128]{0:T(512)(128)(4,1)S(1)}, pred[128]{0:T(512)(128)(4,1)}, u32[]{:S(2)}) copy-start(pred[128]{0:T(512)(128)(4,1)} %compare_or_fusion) | copy-start | bytes 388
  58.0 51.1 %copy-start.11 = (bf16[1,2,2048,352]{2,3,1,0:T(8,128)(2,1)S(1)}, bf16[1,2,2048,352]{2,3,1,0:T(8,128)(2,1)}, u32[]{:S(2)}) copy-start(bf16[1,2,2048,352]{2,3,1,0:T(8,128)(2,1)} %param.28) | copy-start | bytes 8650756
  107.0 2.0 %copy-start.1 = (bf16[2,2,2,2,2,32,2176]{6,5,4,3,2,1,0:T(8,128)(2,1)}, bf16[2,2,2,2,2,32,2176]{6,5,4,3,2,1,0:T(8,128)(2,1)S(1)}, u32[]{:S(2)}) copy-start(bf16[2,2,2,2,2,32,2176]{6,5,4,3,2,1,0:T(8,128)(2,1)S(1)} %shard_map.169) | copy-start | bytes 13369348
  121.3 2.2 %copy-start.2 = (bf16[1024,2048]{1,0:T(8,128)(2,1)S(1)}, bf16[1024,2048]{1,0:T(8,128)(2,1)}, u32[]{:S(2)}) copy-start(bf16[1024,2048]{1,0:T(8,128)(2,1)} %multiply_convert_fusion) | copy-start | bytes 12582916
  166.3 17.9 %copy-start.5 = (bf16[32,2048]{1,0:T(8,128)(2,1)}, bf16[32,2048]{1,0:T(8,128)(2,1)S(1)}, u32[]{:S(2)}) copy-start(bf16[32,2048]{1,0:T(8,128)(2,1)S(1)} %add_convert_fusion) | copy-start | bytes 393220
Sparse Core Ops, SparseCore 0:
  17.8 36.9 all-gather.1

commit v3 on v2

--- a/solution.py
+++ b/solution.py
@@ -160,25 +160,25 @@
     bits = my_bits()
     out_ref[bits] = in_ref[...]
     meet_partners()
+    flying = [None] * len(orders)
     for step in range(5):
-        copies = []
         for p, order in enumerate(orders):
+            if flying[p] is not None:
+                flying[p].wait()
             done = order[:step]
             where = tuple(pl.ds(0, 2) if a in done else bits[a] for a in range(5))
             where = where + (slice(None), pl.ds(*columns[p]))
-            copies.append(
-                pltpu.make_async_remote_copy(
-                    src_ref=out_ref.at[where],
-                    dst_ref=out_ref.at[where],
-                    send_sem=send_sem.at[p, step],
-                    recv_sem=recv_sem.at[p, step],
-                    device_id=partner(order[step]),
-                    device_id_type=pl.DeviceIdType.MESH,
-                )
+            flying[p] = pltpu.make_async_remote_copy(
+                src_ref=out_ref.at[where],
+                dst_ref=out_ref.at[where],
+                send_sem=send_sem.at[p, step],
+                recv_sem=recv_sem.at[p, step],
+                device_id=partner(order[step]),
+                device_id_type=pl.DeviceIdType.MESH,
             )
-            copies[-1].start()
-        for copy in copies:
-            copy.wait()
+            flying[p].start()
+    for copy in flying:
+        copy.wait()
 
 
 def gather_blocks(block, orders, columns, number):
@@ -202,42 +202,48 @@
     bits = my_bits()
     received = (r0, r1, r2, r3, r4)
     meet_partners()
+    flying = [None] * len(orders)
+
+    def take_in(p, step):
+        order = orders[p]
+        held = in_ref if step == 0 else received[step - 1]
+        left = [a for a in range(5) if a not in order[:step]]
+        spot = left.index(order[step])
+        count = len(left) - 1
+        tail = (slice(None), pl.ds(*columns[p]))
+        flying[p].wait()
+
+        def add(i, carry):
+            index = tuple((i // 2 ** (count - 1 - k)) % 2 for k in range(count))
+            mine = index[:spot] + (bits[order[step]],) + index[spot:]
+            total = held[mine + tail].astype(jnp.float32) + received[step][
+                index + tail
+            ].astype(jnp.float32)
+            received[step][index + tail] = total.astype(jnp.bfloat16)
+            return carry
+
+        lax.fori_loop(0, 2**count, add, 0)
+
     for step in range(5):
-        copies = []
         held = in_ref if step == 0 else received[step - 1]
         for p, order in enumerate(orders):
+            if step > 0:
+                take_in(p, step - 1)
             left = [a for a in range(5) if a not in order[:step]]
             give = tuple(1 - bits[a] if a == order[step] else pl.ds(0, 2) for a in left)
             tail = (slice(None), pl.ds(*columns[p]))
             into = tuple(pl.ds(0, 2) for _ in left[1:])
-            copies.append(
-                pltpu.make_async_remote_copy(
-                    src_ref=held.at[give + tail],
-                    dst_ref=received[step].at[into + tail],
-                    send_sem=send_sem.at[p, step],
-                    recv_sem=recv_sem.at[p, step],
-                    device_id=partner(order[step]),
-                    device_id_type=pl.DeviceIdType.MESH,
-                )
+            flying[p] = pltpu.make_async_remote_copy(
+                src_ref=held.at[give + tail],
+                dst_ref=received[step].at[into + tail],
+                send_sem=send_sem.at[p, step],
+                recv_sem=recv_sem.at[p, step],
+                device_id=partner(order[step]),
+                device_id_type=pl.DeviceIdType.MESH,
             )
-            copies[-1].start()
-        for p, order in enumerate(orders):
-            copies[p].wait()
-            left = [a for a in range(5) if a not in order[:step]]
-            spot = left.index(order[step])
-            count = len(left) - 1
-            tail = (slice(None), pl.ds(*columns[p]))
-
-            def add(i, carry):
-                index = tuple((i // 2 ** (count - 1 - k)) % 2 for k in range(count))
-                mine = index[:spot] + (bits[order[step]],) + index[spot:]
-                total = held[mine + tail].astype(jnp.float32) + received[step][
-                    index + tail
-                ].astype(jnp.float32)
-                received[step][index + tail] = total.astype(jnp.bfloat16)
-                return carry
-
-            lax.fori_loop(0, 2**count, add, 0)
+            flying[p].start()
+    for p in range(len(orders)):
+        take_in(p, 4)
     out_ref[...] = received[4][...]
 
 
@@ -272,8 +278,10 @@
     low = (gates - high.astype(jnp.float32)).astype(jnp.bfloat16)
     side = jnp.pad(jnp.concatenate([high, low], axis=1), ((0, 0), (0, 128 - 2 * experts)))
     packed = jnp.concatenate([moe_input, side], axis=1)
-    orders = ((ZLO, ZHI, Y, X, CORE), (ZLO, ZHI, X, Y, CORE))
-    everyone = gather_blocks(packed, orders, ((0, D // 2), (D // 2, D // 2 + 128)), 1)
+    orders = ((ZHI, ZLO, Y, X, CORE), (ZHI, ZLO, X, Y, CORE)) * 2
+    quarter = D // 4
+    columns = tuple((p * quarter, quarter + (128 if p == 3 else 0)) for p in range(4))
+    everyone = gather_blocks(packed, orders, columns, 1)
     everyone = everyone.reshape(-1, D + 128)
     tokens = everyone[:, :D]
     expert = lax.axis_index("dp")
@@ -286,9 +294,10 @@
     hidden = (jax.nn.silu(first) * second).astype(jnp.bfloat16)
     part = jnp.dot(hidden, w_down[0], preferred_element_type=jnp.float32)
     part = (part * gate).astype(jnp.bfloat16)
-    orders = ((CORE, X, Y, ZHI, ZLO), (CORE, Y, X, ZHI, ZLO))
+    orders = ((CORE, X, Y, ZLO, ZHI), (CORE, Y, X, ZLO, ZHI)) * 2
+    columns = tuple((p * quarter, quarter) for p in range(4))
     blocks = part.reshape((2,) * 5 + (rows, D))
-    return scatter_sum(blocks, orders, ((0, D // 2), (D // 2, D // 2)), 2)
+    return scatter_sum(blocks, orders, columns, 2)
 
 
 def per_device(

time: 192 us -> 169 us (0.88)
  Pallas kernels: 107 us -> 83.8 us
    pallas_call x2, Pallas kernels: 64.1 us -> 49.8 us  [gather_blocks(): pl.pallas_call(functools.partial(gather_kernel, orders, columns), out_sha...]
    pallas_call x1, Pallas kernels: 42.7 us -> 34 us  [scatter_sum(): pl.pallas_call(functools.partial(scatter_kernel, orders, columns), out_sh...]
  transfers between devices with their start and end apart: 2 -> 2, of which waited for: 1 -> 1; matrix products, arithmetic and copies ran while one was open for 13% -> 15% of each run, Pallas kernels for 0% -> 0%
where the time goes in v3:
time: 169 us; the launch traced here: 168 us
  Pallas kernels  83.8 us (50%)
  matrix products  23 us (14%)
  local copies, waits for them, and re-layouts  19.8 us (12%)
  between operations  15.7 us (9%)
  blocking collectives  10.4 us (6%)
  waiting for transfers between devices  7.59 us (4%)
  other arithmetic  4.37 us (3%)
  starting transfers between devices  3.41 us (2%)
    pallas_call x2, Pallas kernels, gather_blocks(): pl.pallas_call(functools.partial(gather_kernel, orders, columns), out_sha...  49.8 us
    pallas_call x1, Pallas kernels, scatter_sum(): pl.pallas_call(functools.partial(scatter_kernel, orders, columns), out_sh...  34 us
    all_gather x1, blocking collectives, per_device(): group = lax.all_gather(drafts, 'fsdp', axis=0, tiled=True)  10.4 us
    dot_general x1, matrix products, dense_experts(): part = jnp.dot(hidden, w_down[0], preferred_element_type=jnp.float32)  9.4 us
    unnamed x30, local copies, waits for them, and re-layouts  9.39 us
    all_gather x1, waiting for transfers between devices, per_device(): wide_out = lax.all_gather(w_out, 'fsdp', axis=1, tiled=True)  7.57 us
    slice x1, local copies, waits for them, and re-layouts, attend(): cache_keys = cache_block[0].reshape(slots, HEADS, HD)  3.89 us
  transfers between devices with their start and end apart: 2, of which 1 were waited for; matrix products, arithmetic and copies ran while one was open for 15% of the time, Pallas kernels for 0%

profile of v3, /device:TPU:0, one launch (start us, length us, event | category | flops | bytes accessed | tf_op | source)
XLA Modules:
  0.0 168.1 jit_solution(6014226029418145211)
XLA Ops:
  7.2 10.4 %all_gather.6 = bf16[128,2048]{1,0:T(8,128)(2,1)} all-gather(bf16[32,2048]{1,0:T(8,128)(2,1)} %param.15), channel_id=1, replica_groups=mesh['dp'=8,'fsdp'=4] {'fsdp'}, dimensions={0}, use_global_device_ids=true | all-gather | bytes 655360 | tf_op jit(solution)/shard_map/all_gather | solution.py:323
  17.7 0.8 dynamic_slice.6
  18.5 1.2 fusion.30
  19.7 2.4 %fusion.20 = bf16[128,768]{1,0:T(8,128)(2,1)} fusion(bf16[2048,768]{1,0:T(8,128)(2,1)S(1)} %copy-done, bf16[128,2048]{1,0:T(8,128)(2,1)} %all_gather.6, f32[2048]{0:T(1024)} %param.21, f32[128]{0:T(128)S(1)} %add_rsqrt_fusion.1, f32[768]{0:T(1024)S(1)} %dynamic_slice.6), kind=kOutput, calls=%fused_computation.21 | convolution fusion | flops 403898368 | bytes 3878400 | tf_op jit(solution)/shard_map/dot_general | solution.py:329
  22.1 3.4 %all-to-all-start = ((bf16[4,32,768]{2,1,0:T(8,128)(2,1)}), bf16[4,32,768]{2,1,0:T(8,128)(2,1)S(1)}, u32[]{:S(2)}, u32[]{:S(2)}) async-start(bf16[4,32,768]{2,1,0:T(8,128)(2,1)} %bitcast.1), calls=%async_computation | async-start | bytes 393216 | tf_op jit(solution)/shard_map/all_to_all | solution.py:330
  27.0 0.5 compare_or_fusion
  27.7 0.5 compare_select_fusion
  28.1 0.6 broadcast_add_fusion
  28.7 3.9 %fusion.78 = (bf16[1,1,768,1024]{3,2,1,0:T(8,128)(2,1)}, bf16[1,1,768,1024]{3,2,1,0:T(8,128)(2,1)}) fusion(bf16[1,2,768,1024]{3,2,1,0:T(8,128)(2,1)} %param.16), kind=kLoop, calls=%fused_computation.116 | loop fusion | bytes 6291456 | tf_op jit(solution)/shard_map/vmap()/slice | solution.py:41
  32.6 0.5 fusion.74
  34.0 2.6 %copy.91 = bf16[1,1,768,1024]{2,3,1,0:T(8,128)(2,1)} copy(bf16[1,1,768,1024]{3,2,1,0:T(8,128)(2,1)} %get-tuple-element.33) | data formatting | bytes 3145728
  36.6 2.6 %copy.93 = bf16[1,1,768,1024]{2,3,1,0:T(8,128)(2,1)} copy(bf16[1,1,768,1024]{3,2,1,0:T(8,128)(2,1)} %get-tuple-element.34) | data formatting | bytes 3145728
  39.3 0.8 copy.70
  40.1 1.0 reshape.393
  41.1 0.9 slice_reduce_fusion.1
  42.3 1.9 %fusion.79 = (f32[8,32]{1,0:T(8,128)S(1)}, f32[8,32,768]{2,1,0:T(8,128)S(1)}) fusion(bf16[768,8,128]{0,2,1:T(8,128)(2,1)} %bitcast.105, bf16[1,32,8,1,128]{4,3,2,1,0:T(2,128)(2,1)S(1)} %get-tuple-element.36, pred[768]{0:T(1024)(128)(4,1)S(1)} %iota_compare_fusion.5), kind=kOutput, calls=%fused_computation.117 | convolution fusion | flops 50921216 | bytes 2426624 | tf_op jit(solution)/shard_map/vmap(thd,chd->htc)/dot_general | solution.py:45
  44.2 0.3 fusion.38
  44.5 0.7 convolution_bitcast_fusion
  45.2 0.2 fusion.23
  45.4 0.7 copy.80
  46.5 0.7 maximum_bitcast_fusion
  47.2 7.6 %all-gather.2.cloned.1.call-done = bf16[1024,2048]{1,0:T(8,128)(2,1)} async-done(((bf16[1024,512]{1,0:T(8,128)(2,1)}), bf16[1024,2048]{1,0:T(8,128)(2,1)}) %all-gather.2.cloned.1.call-update) | async-done | bytes 4194320 | tf_op jit(solution)/shard_map/all_gather | solution.py:342
  54.8 3.2 %multiply_reduce_fusion = (f32[32]{0:T(128)S(1)}, f32[32,2048]{1,0:T(8,128)S(1)}) fusion(bf16[1024,2048]{1,0:T(8,128)(2,1)} %all-gather.2.cloned.1.call-done, bf16[4,8,8,128]{3,2,1,0:T(8,128)(2,1)} %bitcast.109, bf16[32,2048]{1,0:T(8,128)(2,1)S(1)} %copy-done.4), kind=kOutput, calls=%fused_computation.56 | convolution fusion | flops 134610912 | bytes 4653184 | tf_op jit(solution)/shard_map/dot_general | solution.py:343
  58.1 1.1 subtract_convert_fusion
  59.3 35.2 %shard_map.169 = bf16[2,2,2,2,2,32,2176]{6,5,4,3,2,1,0:T(8,128)(2,1)S(1)} custom-call(bf16[32,2176]{1,0:T(8,128)(2,1)S(1)} %pad_maximum_fusion.in_ref), custom_call_target="tpu_custom_call" | custom-call | tf_op jit(solution)/shard_map/pallas_call | solution.py:186
  94.7 1.9 %copy-done.1 = bf16[2,2,2,2,2,32,2176]{6,5,4,3,2,1,0:T(8,128)(2,1)} copy-done((bf16[2,2,2,2,2,32,2176]{6,5,4,3,2,1,0:T(8,128)(2,1)}, bf16[2,2,2,2,2,32,2176]{6,5,4,3,2,1,0:T(8,128)(2,1)S(1)}, u32[]{:S(2)}) %copy-start.1) | copy-done | bytes 4456472
  96.5 2.9 %fusion.2 = f32[1024,352]{0,1:T(8,128)} fusion(bf16[1024,2176]{1,0:T(8,128)(2,1)S(1)} %bitcast.100, bf16[1,2,2048,352]{2,3,1,0:T(8,128)(2,1)S(1)} %copy-done.11), kind=kOutput, calls=%fused_computation.4 | convolution fusion | flops 1476395008 | bytes 7077888 | tf_op jit(solution)/shard_map/dot_general | solution.py:292
  99.4 9.4 %multiply_convert_fusion = bf16[1024,2048]{1,0:T(8,128)(2,1)} fusion(f32[1024]{0:T(1024)S(1)} %select_reduce_fusion, bf16[1,352,2048]{2,1,0:T(8,128)(2,1)} %param.29, bf16[1,2,2048,352]{2,3,1,0:T(8,128)(2,1)} %param.28, bf16[1024,2176]{1,0:T(8,128)(2,1)} %bitcast.101, f32[1024,352]{0,1:T(8,128)} %fusion.2), kind=kOutput, calls=%fused_computation.1 | convolution fusion | flops 2959147008 | bytes 12718080 | tf_op jit(solution)/shard_map/dot_general | solution.py:295
  108.8 2.2 %copy-done.2 = bf16[1024,2048]{1,0:T(8,128)(2,1)S(1)} copy-done((bf16[1024,2048]{1,0:T(8,128)(2,1)S(1)}, bf16[1024,2048]{1,0:T(8,128)(2,1)}, u32[]{:S(2)}) %copy-start.2) | copy-done | bytes 4194328
  111.0 34.0 %shard_map.170 = bf16[32,2048]{1,0:T(8,128)(2,1)S(1)} custom-call(bf16[2,2,2,2,2,32,2048]{6,5,4,3,2,1,0:T(8,128)(2,1)S(1)} %bitcast.102), custom_call_target="tpu_custom_call" | custom-call | tf_op jit(solution)/shard_map/pallas_call | solution.py:252
  145.0 14.6 %shard_map.171 = bf16[2,2,2,2,2,16,128]{6,5,4,3,2,1,0:T(8,128)(2,1)S(1)} custom-call(bf16[16,128]{1,0:T(8,128)(2,1)S(1)} %bitcast.104), custom_call_target="tpu_custom_call" | custom-call | tf_op jit(solution)/shard_map/pallas_call | solution.py:186
  159.7 1.5 scatter_custom_fusion
  (56 shorter events, 2.3 us)
Async XLA Ops:
  7.2 12.5 %copy-start = (bf16[2048,768]{1,0:T(8,128)(2,1)S(1)}, bf16[2048,768]{1,0:T(8,128)(2,1)}, u32[]{:S(2)}) copy-start(bf16[2048,768]{1,0:T(8,128)(2,1)} %param.22) | copy-start | bytes 9437188
  7.2 47.6 %all-gather.2.cloned.1.call-start = ((), (), s32[]{:S(2)}) async-start(), calls=%async_computation.1 | async-start | bytes 5242880 | tf_op jit(solution)/shard_map/all_gather | solution.py:342
  17.6 8.5 %copy-start.12 = (s32[1,32]{1,0:T(1,128)S(1)}, s32[1,32]{1,0:T(1,128)}, u32[]{:S(2)}) copy-start(s32[1,32]{1,0:T(1,128)} %param.18) | copy-start | bytes 388
  17.6 9.9 %copy-start.9 = (s32[128,4]{0,1:T(4,128)S(1)}, s32[128,4]{0,1:T(4,128)}, u32[]{:S(2)}) copy-start(s32[128,4]{0,1:T(4,128)} %param.27) | copy-start | bytes 6148
  17.6 10.0 %copy-start.13 = (s32[32]{0:T(128)S(1)}, s32[32]{0:T(128)}, u32[]{:S(2)}) copy-start(s32[32]{0:T(128)} %param.20) | copy-start | bytes 388
  22.1 17.2 %all-to-all-start = ((bf16[4,32,768]{2,1,0:T(8,128)(2,1)}), bf16[4,32,768]{2,1,0:T(8,128)(2,1)S(1)}, u32[]{:S(2)}, u32[]{:S(2)}) async-start(bf16[4,32,768]{2,1,0:T(8,128)(2,1)} %bitcast.1), calls=%async_computation | async-start | bytes 393216 | tf_op jit(solution)/shard_map/all_to_all | solution.py:330
  41.1 3.4 %copy-start.3 = (bf16[1,1,768,1024]{2,3,1,0:T(8,128)(2,1)S(1)}, bf16[1,1,768,1024]{2,3,1,0:T(8,128)(2,1)}, u32[]{:S(2)}) copy-start(bf16[1,1,768,1024]{2,3,1,0:T(8,128)(2,1)} %copy.93) | copy-start | bytes 4718596
  44.2 1.9 %copy-start.7 = (f32[32]{0:T(128)S(1)}, f32[32]{0:T(128)}, u32[]{:S(2)}) copy-start(f32[32]{0:T(128)} %broadcast_add_fusion) | copy-start | bytes 388
  44.2 1.9 %copy-start.8 = (bf16[32]{0:T(256)(128)(2,1)S(1)}, bf16[32]{0:T(256)(128)(2,1)}, u32[]{:S(2)}) copy-start(bf16[32]{0:T(256)(128)(2,1)} %fusion.74) | copy-start | bytes 196
  44.5 10.3 %copy-start.4 = (bf16[32,2048]{1,0:T(8,128)(2,1)S(1)}, bf16[32,2048]{1,0:T(8,128)(2,1)}, u32[]{:S(2)}) copy-start(bf16[32,2048]{1,0:T(8,128)(2,1)} %param.15) | copy-start | bytes 393220
  45.2 12.8 %copy-start.6 = (f32[2048]{0:T(1024)S(1)}, f32[2048]{0:T(1024)}, u32[]{:S(2)}) copy-start(f32[2048]{0:T(1024)} %param.25) | copy-start | bytes 24580
  57.9 36.6 %copy-start.10 = (pred[128]{0:T(512)(128)(4,1)S(1)}, pred[128]{0:T(512)(128)(4,1)}, u32[]{:S(2)}) copy-start(pred[128]{0:T(512)(128)(4,1)} %compare_or_fusion) | copy-start | bytes 388
  58.0 38.5 %copy-start.11 = (bf16[1,2,2048,352]{2,3,1,0:T(8,128)(2,1)S(1)}, bf16[1,2,2048,352]{2,3,1,0:T(8,128)(2,1)}, u32[]{:S(2)}) copy-start(bf16[1,2,2048,352]{2,3,1,0:T(8,128)(2,1)} %param.28) | copy-start | bytes 8650756
  94.5 2.0 %copy-start.1 = (bf16[2,2,2,2,2,32,2176]{6,5,4,3,2,1,0:T(8,128)(2,1)}, bf16[2,2,2,2,2,32,2176]{6,5,4,3,2,1,0:T(8,128)(2,1)S(1)}, u32[]{:S(2)}) copy-start(bf16[2,2,2,2,2,32,2176]{6,5,4,3,2,1,0:T(8,128)(2,1)S(1)} %shard_map.169) | copy-start | bytes 13369348
  108.8 2.2 %copy-start.2 = (bf16[1024,2048]{1,0:T(8,128)(2,1)S(1)}, bf16[1024,2048]{1,0:T(8,128)(2,1)}, u32[]{:S(2)}) copy-start(bf16[1024,2048]{1,0:T(8,128)(2,1)} %multiply_convert_fusion) | copy-start | bytes 12582916
  145.0 16.3 %copy-start.5 = (bf16[32,2048]{1,0:T(8,128)(2,1)}, bf16[32,2048]{1,0:T(8,128)(2,1)S(1)}, u32[]{:S(2)}) copy-start(bf16[32,2048]{1,0:T(8,128)(2,1)S(1)} %add_convert_fusion) | copy-start | bytes 393220
Sparse Core Ops, SparseCore 0:
  17.8 36.9 all-gather.1

commit v4 on v3

--- a/solution.py
+++ b/solution.py
@@ -321,7 +321,6 @@
     requests = cache.shape[0]
     feature = HEADS * HD
     group = lax.all_gather(drafts, "fsdp", axis=0, tiled=True)
-    w_out, group = lax.optimization_barrier((w_out, group))
     normed = scaled_norm(group, attn_gain)
     columns = w_qkv.shape[1]
     mine = lax.axis_index("fsdp") * columns

time: 169 us -> 163 us (0.964)
  waiting for transfers between devices: 7.59 us -> 4.48 us
    all_gather x1, waiting for transfers between devices: 7.57 us -> 3.8 us  [per_device(): wide_out = lax.all_gather(w_out, 'fsdp', axis=1, tiled=True)]
  transfers between devices with their start and end apart: 2 -> 2, of which waited for: 1 -> 1; matrix products, arithmetic and copies ran while one was open for 15% -> 14% of each run, Pallas kernels for 0% -> 0%
where the time goes in v4:
time: 163 us; the launch traced here: 162 us
  Pallas kernels  83.8 us (51%)
  matrix products  22.6 us (14%)
  local copies, waits for them, and re-layouts  20 us (12%)
  between operations  15.7 us (10%)
  blocking collectives  8.95 us (5%)
  waiting for transfers between devices  4.48 us (3%)
  starting transfers between devices  3.4 us (2%)
  other arithmetic  3.33 us (2%)
    pallas_call x2, Pallas kernels, gather_blocks(): pl.pallas_call(functools.partial(gather_kernel, orders, columns), out_sha...  49.9 us
    pallas_call x1, Pallas kernels, scatter_sum(): pl.pallas_call(functools.partial(scatter_kernel, orders, columns), out_sh...  34 us
    dot_general x1, matrix products, dense_experts(): part = jnp.dot(hidden, w_down[0], preferred_element_type=jnp.float32)  9.4 us
    unnamed x30, local copies, waits for them, and re-layouts  9.33 us
    all_gather x1, blocking collectives, per_device(): group = lax.all_gather(drafts, 'fsdp', axis=0, tiled=True)  8.95 us
    slice x1, local copies, waits for them, and re-layouts, attend(): cache_keys = cache_block[0].reshape(slots, HEADS, HD)  3.89 us
    all_gather x1, waiting for transfers between devices, per_device(): wide_out = lax.all_gather(w_out, 'fsdp', axis=1, tiled=True)  3.8 us
    all_to_all x1, starting transfers between devices, per_device(): lax.all_to_all(part_qkv, 'fsdp', split_axis=0, concat_axis=1, tiled=True)  3.36 us
  transfers between devices with their start and end apart: 2, of which 1 were waited for; matrix products, arithmetic and copies ran while one was open for 14% of the time, Pallas kernels for 0%

profile of v4, /device:TPU:0, one launch (start us, length us, event | category | flops | bytes accessed | tf_op | source)
XLA Modules:
  0.0 162.2 jit_solution(6322380088452040290)
XLA Ops:
  7.2 0.7 all-gather.2.cloned.1.call-update
  7.9 1.0 dynamic_slice.6
  8.9 8.9 %all_gather.6 = bf16[128,2048]{1,0:T(8,128)(2,1)S(1)} all-gather(bf16[32,2048]{1,0:T(8,128)(2,1)} %param.15), channel_id=1, replica_groups=mesh['dp'=8,'fsdp'=4] {'fsdp'}, dimensions={0}, use_global_device_ids=true | all-gather | bytes 655360 | tf_op jit(solution)/shard_map/all_gather | solution.py:323
  18.1 2.0 %fusion.20 = bf16[128,768]{1,0:T(8,128)(2,1)} fusion(bf16[2048,768]{1,0:T(8,128)(2,1)S(1)} %copy-done, bf16[128,2048]{1,0:T(8,128)(2,1)S(1)} %all_gather.6, f32[2048]{0:T(1024)} %param.21, f32[128]{0:T(128)S(1)} %add_rsqrt_fusion.1, f32[768]{0:T(1024)S(1)} %dynamic_slice.6), kind=kOutput, calls=%fused_computation.21 | convolution fusion | flops 403898368 | bytes 3878400 | tf_op jit(solution)/shard_map/dot_general | solution.py:328
  20.1 3.4 %all-to-all-start = ((bf16[4,32,768]{2,1,0:T(8,128)(2,1)}), bf16[4,32,768]{2,1,0:T(8,128)(2,1)S(1)}, u32[]{:S(2)}, u32[]{:S(2)}) async-start(bf16[4,32,768]{2,1,0:T(8,128)(2,1)} %bitcast.1), calls=%async_computation | async-start | bytes 393216 | tf_op jit(solution)/shard_map/all_to_all | solution.py:329
  25.1 0.5 compare_or_fusion
  25.7 0.5 compare_select_fusion
  26.2 0.6 broadcast_add_fusion
  26.7 3.9 %fusion.78 = (bf16[1,1,768,1024]{3,2,1,0:T(8,128)(2,1)}, bf16[1,1,768,1024]{3,2,1,0:T(8,128)(2,1)}) fusion(bf16[1,2,768,1024]{3,2,1,0:T(8,128)(2,1)} %param.16), kind=kLoop, calls=%fused_computation.116 | loop fusion | bytes 6291456 | tf_op jit(solution)/shard_map/vmap()/slice | solution.py:41
  30.6 0.5 fusion.74
  32.0 2.6 %copy.91 = bf16[1,1,768,1024]{2,3,1,0:T(8,128)(2,1)} copy(bf16[1,1,768,1024]{3,2,1,0:T(8,128)(2,1)} %get-tuple-element.29) | data formatting | bytes 3145728
  34.6 2.6 %copy.93 = bf16[1,1,768,1024]{2,3,1,0:T(8,128)(2,1)} copy(bf16[1,1,768,1024]{3,2,1,0:T(8,128)(2,1)} %get-tuple-element.30) | data formatting | bytes 3145728
  37.2 0.8 copy.70
  38.1 1.0 reshape.393
  39.1 0.9 slice_reduce_fusion.1
  40.2 1.8 %fusion.79 = (f32[8,32]{1,0:T(8,128)S(1)}, f32[8,32,768]{2,1,0:T(8,128)S(1)}) fusion(bf16[768,8,128]{0,2,1:T(8,128)(2,1)} %bitcast.105, bf16[1,32,8,1,128]{4,3,2,1,0:T(2,128)(2,1)S(1)} %get-tuple-element.32, pred[768]{0:T(1024)(128)(4,1)S(1)} %iota_compare_fusion.5), kind=kOutput, calls=%fused_computation.117 | convolution fusion | flops 50921216 | bytes 2426624 | tf_op jit(solution)/shard_map/vmap(thd,chd->htc)/dot_general | solution.py:45
  42.1 0.3 fusion.38
  42.4 0.7 convolution_bitcast_fusion
  43.1 0.2 fusion.23
  43.3 0.7 copy.80
  44.4 0.7 maximum_bitcast_fusion
  45.1 3.8 %all-gather.2.cloned.1.call-done = bf16[1024,2048]{1,0:T(8,128)(2,1)} async-done(((bf16[1024,512]{1,0:T(8,128)(2,1)}), bf16[1024,2048]{1,0:T(8,128)(2,1)}) %all-gather.2.cloned.1.call-update) | async-done | bytes 4194320 | tf_op jit(solution)/shard_map/all_gather | solution.py:341
  48.9 3.2 %multiply_reduce_fusion = (f32[32]{0:T(128)S(1)}, f32[32,2048]{1,0:T(8,128)S(1)}) fusion(bf16[1024,2048]{1,0:T(8,128)(2,1)} %all-gather.2.cloned.1.call-done, bf16[4,8,8,128]{3,2,1,0:T(8,128)(2,1)} %bitcast.109, bf16[32,2048]{1,0:T(8,128)(2,1)S(1)} %copy-done.4), kind=kOutput, calls=%fused_computation.56 | convolution fusion | flops 134610912 | bytes 4653184 | tf_op jit(solution)/shard_map/dot_general | solution.py:342
  52.2 1.1 subtract_convert_fusion
  53.4 35.2 %shard_map.169 = bf16[2,2,2,2,2,32,2176]{6,5,4,3,2,1,0:T(8,128)(2,1)S(1)} custom-call(bf16[32,2176]{1,0:T(8,128)(2,1)S(1)} %pad_maximum_fusion.in_ref), custom_call_target="tpu_custom_call" | custom-call | tf_op jit(solution)/shard_map/pallas_call | solution.py:186
  88.8 1.9 %copy-done.1 = bf16[2,2,2,2,2,32,2176]{6,5,4,3,2,1,0:T(8,128)(2,1)} copy-done((bf16[2,2,2,2,2,32,2176]{6,5,4,3,2,1,0:T(8,128)(2,1)}, bf16[2,2,2,2,2,32,2176]{6,5,4,3,2,1,0:T(8,128)(2,1)S(1)}, u32[]{:S(2)}) %copy-start.1) | copy-done | bytes 4456472
  90.7 2.9 %fusion.2 = f32[1024,352]{0,1:T(8,128)} fusion(bf16[1024,2176]{1,0:T(8,128)(2,1)S(1)} %bitcast.100, bf16[1,2,2048,352]{2,3,1,0:T(8,128)(2,1)S(1)} %copy-done.11), kind=kOutput, calls=%fused_computation.4 | convolution fusion | flops 1476395008 | bytes 7077888 | tf_op jit(solution)/shard_map/dot_general | solution.py:292
  93.5 9.4 %multiply_convert_fusion = bf16[1024,2048]{1,0:T(8,128)(2,1)} fusion(f32[1024]{0:T(1024)S(1)} %select_reduce_fusion, bf16[1,352,2048]{2,1,0:T(8,128)(2,1)} %param.29, bf16[1,2,2048,352]{2,3,1,0:T(8,128)(2,1)} %param.28, bf16[1024,2176]{1,0:T(8,128)(2,1)} %bitcast.101, f32[1024,352]{0,1:T(8,128)} %fusion.2), kind=kOutput, calls=%fused_computation.1 | convolution fusion | flops 2959147008 | bytes 12718080 | tf_op jit(solution)/shard_map/dot_general | solution.py:295
  102.9 2.2 %copy-done.2 = bf16[1024,2048]{1,0:T(8,128)(2,1)S(1)} copy-done((bf16[1024,2048]{1,0:T(8,128)(2,1)S(1)}, bf16[1024,2048]{1,0:T(8,128)(2,1)}, u32[]{:S(2)}) %copy-start.2) | copy-done | bytes 4194328
  105.1 34.0 %shard_map.170 = bf16[32,2048]{1,0:T(8,128)(2,1)S(1)} custom-call(bf16[2,2,2,2,2,32,2048]{6,5,4,3,2,1,0:T(8,128)(2,1)S(1)} %bitcast.102), custom_call_target="tpu_custom_call" | custom-call | tf_op jit(solution)/shard_map/pallas_call | solution.py:252
  139.2 14.6 %shard_map.171 = bf16[2,2,2,2,2,16,128]{6,5,4,3,2,1,0:T(8,128)(2,1)S(1)} custom-call(bf16[16,128]{1,0:T(8,128)(2,1)S(1)} %bitcast.104), custom_call_target="tpu_custom_call" | custom-call | tf_op jit(solution)/shard_map/pallas_call | solution.py:186
  153.8 1.5 scatter_custom_fusion
  (56 shorter events, 2.5 us)
Async XLA Ops:
  7.2 10.9 %copy-start = (bf16[2048,768]{1,0:T(8,128)(2,1)S(1)}, bf16[2048,768]{1,0:T(8,128)(2,1)}, u32[]{:S(2)}) copy-start(bf16[2048,768]{1,0:T(8,128)(2,1)} %param.22) | copy-start | bytes 9437188
  7.2 41.7 %all-gather.2.cloned.1.call-start = ((), (), s32[]{:S(2)}) async-start(), calls=%async_computation.1 | async-start | bytes 5242880 | tf_op jit(solution)/shard_map/all_gather | solution.py:341
  7.9 16.2 %copy-start.12 = (s32[1,32]{1,0:T(1,128)S(1)}, s32[1,32]{1,0:T(1,128)}, u32[]{:S(2)}) copy-start(s32[1,32]{1,0:T(1,128)} %param.18) | copy-start | bytes 388
  8.9 16.7 %copy-start.9 = (s32[128,4]{0,1:T(4,128)S(1)}, s32[128,4]{0,1:T(4,128)}, u32[]{:S(2)}) copy-start(s32[128,4]{0,1:T(4,128)} %param.27) | copy-start | bytes 6148
  8.9 16.8 %copy-start.13 = (s32[32]{0:T(128)S(1)}, s32[32]{0:T(128)}, u32[]{:S(2)}) copy-start(s32[32]{0:T(128)} %param.20) | copy-start | bytes 388
  20.1 17.1 %all-to-all-start = ((bf16[4,32,768]{2,1,0:T(8,128)(2,1)}), bf16[4,32,768]{2,1,0:T(8,128)(2,1)S(1)}, u32[]{:S(2)}, u32[]{:S(2)}) async-start(bf16[4,32,768]{2,1,0:T(8,128)(2,1)} %bitcast.1), calls=%async_computation | async-start | bytes 393216 | tf_op jit(solution)/shard_map/all_to_all | solution.py:329
  39.1 3.4 %copy-start.3 = (bf16[1,1,768,1024]{2,3,1,0:T(8,128)(2,1)S(1)}, bf16[1,1,768,1024]{2,3,1,0:T(8,128)(2,1)}, u32[]{:S(2)}) copy-start(bf16[1,1,768,1024]{2,3,1,0:T(8,128)(2,1)} %copy.93) | copy-start | bytes 4718596
  42.1 1.9 %copy-start.7 = (f32[32]{0:T(128)S(1)}, f32[32]{0:T(128)}, u32[]{:S(2)}) copy-start(f32[32]{0:T(128)} %broadcast_add_fusion) | copy-start | bytes 388
  42.1 1.9 %copy-start.8 = (bf16[32]{0:T(256)(128)(2,1)S(1)}, bf16[32]{0:T(256)(128)(2,1)}, u32[]{:S(2)}) copy-start(bf16[32]{0:T(256)(128)(2,1)} %fusion.74) | copy-start | bytes 196
  42.4 6.5 %copy-start.4 = (bf16[32,2048]{1,0:T(8,128)(2,1)S(1)}, bf16[32,2048]{1,0:T(8,128)(2,1)}, u32[]{:S(2)}) copy-start(bf16[32,2048]{1,0:T(8,128)(2,1)} %param.15) | copy-start | bytes 393220
  43.1 9.0 %copy-start.6 = (f32[2048]{0:T(1024)S(1)}, f32[2048]{0:T(1024)}, u32[]{:S(2)}) copy-start(f32[2048]{0:T(1024)} %param.25) | copy-start | bytes 24580
  52.1 36.6 %copy-start.10 = (pred[128]{0:T(512)(128)(4,1)S(1)}, pred[128]{0:T(512)(128)(4,1)}, u32[]{:S(2)}) copy-start(pred[128]{0:T(512)(128)(4,1)} %compare_or_fusion) | copy-start | bytes 388
  52.1 38.5 %copy-start.11 = (bf16[1,2,2048,352]{2,3,1,0:T(8,128)(2,1)S(1)}, bf16[1,2,2048,352]{2,3,1,0:T(8,128)(2,1)}, u32[]{:S(2)}) copy-start(bf16[1,2,2048,352]{2,3,1,0:T(8,128)(2,1)} %param.28) | copy-start | bytes 8650756
  88.6 2.0 %copy-start.1 = (bf16[2,2,2,2,2,32,2176]{6,5,4,3,2,1,0:T(8,128)(2,1)}, bf16[2,2,2,2,2,32,2176]{6,5,4,3,2,1,0:T(8,128)(2,1)S(1)}, u32[]{:S(2)}) copy-start(bf16[2,2,2,2,2,32,2176]{6,5,4,3,2,1,0:T(8,128)(2,1)S(1)} %shard_map.169) | copy-start | bytes 13369348
  102.9 2.2 %copy-start.2 = (bf16[1024,2048]{1,0:T(8,128)(2,1)S(1)}, bf16[1024,2048]{1,0:T(8,128)(2,1)}, u32[]{:S(2)}) copy-start(bf16[1024,2048]{1,0:T(8,128)(2,1)} %multiply_convert_fusion) | copy-start | bytes 12582916
  139.1 16.3 %copy-start.5 = (bf16[32,2048]{1,0:T(8,128)(2,1)}, bf16[32,2048]{1,0:T(8,128)(2,1)S(1)}, u32[]{:S(2)}) copy-start(bf16[32,2048]{1,0:T(8,128)(2,1)S(1)} %add_convert_fusion) | copy-start | bytes 393220
Sparse Core Ops, SparseCore 0:
  9.6 39.2 all-gather.1
